TPU v7x, 256 devices: a whole 4x4x8 slice. The times are simulated.
256 devices in a mesh: gx: 8 (over z), gy: 8 (over y, core), gz: 4 (over x).
Axes of the slice: x: 4, y: 4, z: 8, core: 2. Of those that a mesh axis runs over, the one named last changes fastest.
Arguments:
- right_side: float32 [128, 128, 512], P('gx', 'gy', 'gz'), may hold values from -10 to 10
- initial: float32 [128, 128, 512], P('gx', 'gy', 'gz'), may hold values from -8 to 8
- shift: float32 [128, 128, 512], P('gx', 'gy', 'gz'), may hold values from 0.05 to 0.5
- beta: float32 [128, 128, 512], P('gx', 'gy', 'gz'), may hold values from 0.5 to 5
Outputs:
- solution_field: float32 [128, 128, 512], P('gx', 'gy', 'gz')
- residual: float32 [128, 128, 512], P('gx', 'gy', 'gz')
All inputs are finite; a program needn't handle non-finite values.
Results may differ from a plain program's by a relative error of at most 0.0003.
Values sent between devices are 32-bit elements; how exact they have to be, the bound alone decides.
A program may use at most 128 MiB of HBM per device.

v0:
```python
import jax
import jax.numpy as jnp
from jax import lax
from jax.sharding import PartitionSpec as P

SWEEPS = 2
CG_ITERS = 8


def with_halo(block, sides, width):
    for axis, dim in sides:
        count = lax.axis_size(axis)
        forward = [(i, i + 1) for i in range(count - 1)]
        backward = [(target, source) for source, target in forward]
        low = lax.ppermute(
            lax.slice_in_dim(block, block.shape[dim] - width, None, axis=dim), axis, forward
        )
        high = lax.ppermute(lax.slice_in_dim(block, 0, width, axis=dim), axis, backward)
        block = jnp.concatenate([low, block, high], axis=dim)
    return block


def face_weights(padded):
    center = padded[1:-1, 1:-1, 1:-1]
    return (
        0.5 * (center + padded[2:, 1:-1, 1:-1]),
        0.5 * (center + padded[:-2, 1:-1, 1:-1]),
        0.5 * (center + padded[1:-1, 2:, 1:-1]),
        0.5 * (center + padded[1:-1, :-2, 1:-1]),
        0.5 * (center + padded[1:-1, 1:-1, 2:]),
        0.5 * (center + padded[1:-1, 1:-1, :-2]),
    )


def nearby(padded):
    return (
        padded[2:, 1:-1, 1:-1],
        padded[:-2, 1:-1, 1:-1],
        padded[1:-1, 2:, 1:-1],
        padded[1:-1, :-2, 1:-1],
        padded[1:-1, 1:-1, 2:],
        padded[1:-1, 1:-1, :-2],
    )


def relax_core(padded, source, shift_term, weight_list, scale):
    values = nearby(padded)
    upper_sum = weight_list[0] * values[0]
    lower_sum = weight_list[0]
    for position in range(1, 6):
        upper_sum = upper_sum + weight_list[position] * values[position]
        lower_sum = lower_sum + weight_list[position]
    return (source + scale * upper_sum) / (shift_term + scale * lower_sum)


def operate(padded, shift_term, weight_list, scale):
    center = padded[1:-1, 1:-1, 1:-1]
    values = nearby(padded)
    total = weight_list[0] * (center - values[0])
    for position in range(1, 6):
        total = total + weight_list[position] * (center - values[position])
    return shift_term * center + scale * total


def parity(shape):
    first_index = lax.broadcasted_iota(jnp.int32, shape, 0)
    second_index = lax.broadcasted_iota(jnp.int32, shape, 1)
    third_index = lax.broadcasted_iota(jnp.int32, shape, 2)
    return (first_index + second_index + third_index) % 2 == 0


def restrict(values):
    size_a, size_b, size_c = values.shape
    return values.reshape(size_a // 2, 2, size_b // 2, 2, size_c // 2, 2).mean(axis=(1, 3, 5))


def prolong(values):
    return jnp.repeat(jnp.repeat(jnp.repeat(values, 2, axis=0), 2, axis=1), 2, axis=2)


def faces(values):
    return with_halo(values, (("gx", 0), ("gy", 1), ("gz", 2)), 1)


def level_data(beta_level):
    return (face_weights(faces(beta_level)), None)


def smooth_level(field, source, shift_level, inner, scale):
    red = parity(field.shape)
    for repeat_index in range(SWEEPS):
        for colour in (red, jnp.logical_not(red)):
            field = jnp.where(
                colour, relax_core(faces(field), source, shift_level, inner, scale), field
            )
    return field


def global_norm(values):
    return lax.psum(jnp.sum(values * values), ("gx", "gy", "gz"))


def global_curvature(direction, image):
    return lax.psum(jnp.sum(direction * image), ("gx", "gy", "gz"))


def local(right_side, initial, shift, beta):
    shift_one = restrict(shift)
    shift_two = restrict(shift_one)
    beta_one = restrict(beta)
    beta_two = restrict(beta_one)
    inner_zero, outer_zero = level_data(beta)
    pre_zero = smooth_level(initial, right_side, shift, inner_zero, 1.0)
    source_one = restrict(right_side - operate(faces(pre_zero), shift, inner_zero, 1.0))
    inner_one, outer_one = level_data(beta_one)
    pre_one = smooth_level(jnp.zeros_like(source_one), source_one, shift_one, inner_one, 0.25)
    source_two = restrict(source_one - operate(faces(pre_one), shift_one, inner_one, 0.25))
    weights_two = face_weights(faces(beta_two))
    bottom = jnp.zeros_like(source_two)
    remain = source_two
    direction = source_two
    norm_now = global_norm(remain)
    for repeat_index in range(CG_ITERS):
        image = operate(faces(direction), shift_two, weights_two, 0.0625)
        step_size = norm_now / global_curvature(direction, image)
        bottom = bottom + step_size * direction
        remain = remain - step_size * image
        norm_next = global_norm(remain)
        direction = remain + norm_next / norm_now * direction
        norm_now = norm_next
    post_one = smooth_level(pre_one + prolong(bottom), source_one, shift_one, inner_one, 0.25)
    solution_field = smooth_level(pre_zero + prolong(post_one), right_side, shift, inner_zero, 1.0)
    residual = right_side - operate(faces(solution_field), shift, inner_zero, 1.0)
    return (solution_field, residual)


def solution(mesh):
    in_specs = (P("gx", "gy", "gz"), P("gx", "gy", "gz"), P("gx", "gy", "gz"), P("gx", "gy", "gz"))
    out_specs = (P("gx", "gy", "gz"), P("gx", "gy", "gz"))
    return jax.shard_map(local, mesh=mesh, in_specs=in_specs, out_specs=out_specs, check_vma=False)
```

profile of v0, /device:TPU:1, one launch (start us, length us, event | category | flops | bytes accessed | tf_op | source)
XLA Modules:
  0.0 1906.2 jit_solution(11671991638991541659)
XLA Ops:
  1.4 4.4 collective-permute-start.3
  16.6 5.3 collective-permute-start.7
  39.3 4.6 collective-permute-start.11
  51.0 4.7 collective-permute-start.13
  60.7 5.1 collective-permute-start.15
  81.7 4.8 collective-permute-start.19
  87.9 4.4 collective-permute-start.39
  93.6 9.7 reshape.43
  118.1 4.8 collective-permute-start.23
  122.9 4.6 collective-permute-start.38
  127.5 9.7 reshape.44
  181.4 4.4 collective-permute-start.47
  185.9 4.5 collective-permute-start.33
  206.3 9.7 reshape.42
  220.3 4.7 collective-permute-start.49
  226.3 4.5 collective-permute-done.48
  230.8 4.7 collective-permute-start.51
  241.9 4.7 collective-permute-start.53
  248.2 4.8 collective-permute-start.55
  254.4 4.5 collective-permute-done.54
  269.3 4.6 collective-permute-start.59
  275.5 4.8 collective-permute-start.61
  295.3 4.6 collective-permute-start.65
  307.8 4.6 collective-permute-start.74
  322.5 4.6 collective-permute-start.71
  340.9 4.9 collective-permute-start.79
  354.2 4.9 collective-permute-start.83
  360.8 77.2 %all-reduce.2 = (f32[]{:T(128)}, f32[]{:T(128)}) all-reduce(f32[]{:T(128)} %get-tuple-element.11, f32[]{:T(128)} %get-tuple-element.10), channel_id=1, replica_groups=mesh['gx'=8,'gy'=8,'gz'=4] {'gx','gy','gz'}, use_global_device_ids=true, to_apply=%region_5.6 | all-reduce | flops 2 | bytes 16 | tf_op jit(solution)/shard_map/psum | solution.py:100
  439.9 73.5 %psum.114 = f32[]{:T(128)} all-reduce(f32[]{:T(128)} %multiply_reduce_fusion.12), channel_id=1, replica_groups=mesh['gx'=8,'gy'=8,'gz'=4] {'gx','gy','gz'}, use_global_device_ids=true, to_apply=%region_11.12 | all-reduce | flops 1 | bytes 8 | tf_op jit(solution)/shard_map/psum | solution.py:100
  522.8 5.0 collective-permute-start.87
  539.7 74.9 %psum.115 = f32[]{:T(128)} all-reduce(f32[]{:T(128)} %get-tuple-element.34), channel_id=1, replica_groups=mesh['gx'=8,'gy'=8,'gz'=4] {'gx','gy','gz'}, use_global_device_ids=true, to_apply=%region_13.14 | all-reduce | flops 1 | bytes 8 | tf_op jit(solution)/shard_map/psum | solution.py:104
  616.6 72.8 %psum.116 = f32[]{:T(128)} all-reduce(f32[]{:T(128)} %get-tuple-element.32), channel_id=1, replica_groups=mesh['gx'=8,'gy'=8,'gz'=4] {'gx','gy','gz'}, use_global_device_ids=true, to_apply=%region_15.16 | all-reduce | flops 1 | bytes 8 | tf_op jit(solution)/shard_map/psum | solution.py:100
  698.7 4.8 collective-permute-start.93
  715.5 74.9 %psum.117 = f32[]{:T(128)} all-reduce(f32[]{:T(128)} %get-tuple-element.30), channel_id=1, replica_groups=mesh['gx'=8,'gy'=8,'gz'=4] {'gx','gy','gz'}, use_global_device_ids=true, to_apply=%region_17.18 | all-reduce | flops 1 | bytes 8 | tf_op jit(solution)/shard_map/psum | solution.py:104
  792.4 72.8 %psum.118 = f32[]{:T(128)} all-reduce(f32[]{:T(128)} %get-tuple-element.28), channel_id=1, replica_groups=mesh['gx'=8,'gy'=8,'gz'=4] {'gx','gy','gz'}, use_global_device_ids=true, to_apply=%region_19.20 | all-reduce | flops 1 | bytes 8 | tf_op jit(solution)/shard_map/psum | solution.py:100
  874.5 4.8 collective-permute-start.99
  891.3 75.1 %psum.119 = f32[]{:T(128)} all-reduce(f32[]{:T(128)} %get-tuple-element.26), channel_id=1, replica_groups=mesh['gx'=8,'gy'=8,'gz'=4] {'gx','gy','gz'}, use_global_device_ids=true, to_apply=%region_21.22 | all-reduce | flops 1 | bytes 8 | tf_op jit(solution)/shard_map/psum | solution.py:104
  968.3 72.8 %psum.120 = f32[]{:T(128)} all-reduce(f32[]{:T(128)} %get-tuple-element.24), channel_id=1, replica_groups=mesh['gx'=8,'gy'=8,'gz'=4] {'gx','gy','gz'}, use_global_device_ids=true, to_apply=%region_23.24 | all-reduce | flops 1 | bytes 8 | tf_op jit(solution)/shard_map/psum | solution.py:100
  1050.5 4.8 collective-permute-start.105
  1067.3 74.9 %psum.121 = f32[]{:T(128)} all-reduce(f32[]{:T(128)} %get-tuple-element.22), channel_id=1, replica_groups=mesh['gx'=8,'gy'=8,'gz'=4] {'gx','gy','gz'}, use_global_device_ids=true, to_apply=%region_25.26 | all-reduce | flops 1 | bytes 8 | tf_op jit(solution)/shard_map/psum | solution.py:104
  1144.2 72.8 %psum.122 = f32[]{:T(128)} all-reduce(f32[]{:T(128)} %get-tuple-element.20), channel_id=1, replica_groups=mesh['gx'=8,'gy'=8,'gz'=4] {'gx','gy','gz'}, use_global_device_ids=true, to_apply=%region_27.28 | all-reduce | flops 1 | bytes 8 | tf_op jit(solution)/shard_map/psum | solution.py:100
  1226.3 4.8 collective-permute-start.111
  1243.1 74.9 %psum.123 = f32[]{:T(128)} all-reduce(f32[]{:T(128)} %get-tuple-element.18), channel_id=1, replica_groups=mesh['gx'=8,'gy'=8,'gz'=4] {'gx','gy','gz'}, use_global_device_ids=true, to_apply=%region_29.30 | all-reduce | flops 1 | bytes 8 | tf_op jit(solution)/shard_map/psum | solution.py:104
  1320.0 72.8 %psum.124 = f32[]{:T(128)} all-reduce(f32[]{:T(128)} %get-tuple-element.16), channel_id=1, replica_groups=mesh['gx'=8,'gy'=8,'gz'=4] {'gx','gy','gz'}, use_global_device_ids=true, to_apply=%region_31.32 | all-reduce | flops 1 | bytes 8 | tf_op jit(solution)/shard_map/psum | solution.py:100
  1402.2 4.8 collective-permute-start.117
  1418.9 74.9 %psum.125 = f32[]{:T(128)} all-reduce(f32[]{:T(128)} %get-tuple-element.14), channel_id=1, replica_groups=mesh['gx'=8,'gy'=8,'gz'=4] {'gx','gy','gz'}, use_global_device_ids=true, to_apply=%region_33.34 | all-reduce | flops 1 | bytes 8 | tf_op jit(solution)/shard_map/psum | solution.py:104
  1495.8 72.8 %psum.126 = f32[]{:T(128)} all-reduce(f32[]{:T(128)} %multiply_reduce_fusion), channel_id=1, replica_groups=mesh['gx'=8,'gy'=8,'gz'=4] {'gx','gy','gz'}, use_global_device_ids=true, to_apply=%region_35.36 | all-reduce | flops 1 | bytes 8 | tf_op jit(solution)/shard_map/psum | solution.py:100
  1578.0 4.8 collective-permute-start.123
  1594.7 74.9 %psum.127 = f32[]{:T(128)} all-reduce(f32[]{:T(128)} %fusion.483), channel_id=1, replica_groups=mesh['gx'=8,'gy'=8,'gz'=4] {'gx','gy','gz'}, use_global_device_ids=true, to_apply=%region_37.38 | all-reduce | flops 1 | bytes 8 | tf_op jit(solution)/shard_map/psum | solution.py:104
  1701.1 4.6 collective-permute-start.135
  1712.1 4.7 collective-permute-start.137
  1718.4 4.8 collective-permute-start.139
  1727.9 4.4 collective-permute-start.141
  1738.7 4.7 collective-permute-start.143
  1753.1 4.3 collective-permute-start.147
  1763.7 5.0 collective-permute-start.149
  1778.2 4.6 collective-permute-start.153
  1789.3 4.7 collective-permute-start.155
  1805.4 5.7 collective-permute-start.159
  1817.5 4.7 collective-permute-start.161
  1833.6 4.8 collective-permute-start.165
  1844.9 4.7 collective-permute-start.167
  1870.7 4.7 collective-permute-start.173
  1896.6 4.7 collective-permute-start.179
  (518 shorter events, 522.8 us)
Async XLA Ops:
  1.4 11.2 collective-permute-start.3
  6.5 17.3 collective-permute-start.2
  10.0 14.7 collective-permute-start
  16.6 13.8 collective-permute-start.7
  21.8 8.5 collective-permute-start.5
  33.6 10.4 collective-permute-start.10
  36.7 9.4 collective-permute-start.8
  38.0 11.3 collective-permute-start.9
  39.3 10.0 collective-permute-start.11
  60.7 7.0 collective-permute-start.15
  70.9 7.6 collective-permute-start.16
  72.2 8.1 collective-permute-start.17
  81.7 25.7 %collective-permute-start.19 = (f32[1,16,128]{2,1,0:T(8,128)S(1)}, f32[1,16,128]{2,1,0:T(8,128)S(1)}, u32[]{:S(2)}, u32[]{:S(2)}) collective-permute-start(f32[1,16,128]{2,1,0:T(8,128)S(1)} %get-tuple-element.109), channel_id=1, source_target_pairs={{0,32},{32,64},{64,96},{96,128},{128,160},{160,192},{192,224},{1,3... | collective-permute-start | bytes 24584 | tf_op jit(solution)/shard_map/ppermute | solution.py:15
  86.6 20.8 %collective-permute-start.18 = (f32[1,16,128]{2,1,0:T(8,128)S(1)}, f32[1,16,128]{2,1,0:T(8,128)S(1)}, u32[]{:S(2)}, u32[]{:S(2)}) collective-permute-start(f32[1,16,128]{2,1,0:T(8,128)S(1)} %get-tuple-element.110), channel_id=1, source_target_pairs={{32,0},{64,32},{96,64},{128,96},{160,128},{192,160},{224,192},{33,... | collective-permute-start | bytes 24584 | tf_op jit(solution)/shard_map/ppermute | solution.py:18
  87.9 59.3 %collective-permute-start.39 = (f32[1,8,64]{2,1,0:T(8,128)S(1)}, f32[1,8,64]{2,1,0:T(8,128)S(1)}, u32[]{:S(2)}, u32[]{:S(2)}) collective-permute-start(f32[1,8,64]{2,1,0:T(8,128)S(1)} %broadcast.62), channel_id=1, source_target_pairs={{0,32},{32,64},{64,96},{96,128},{128,160},{160,192},{192,224},{1,3... | collective-permute-start | bytes 6152 | tf_op jit(solution)/shard_map/ppermute | solution.py:15
  92.3 56.2 %collective-permute-start.37 = (f32[1,8,64]{2,1,0:T(8,128)S(1)}, f32[1,8,64]{2,1,0:T(8,128)S(1)}, u32[]{:S(2)}, u32[]{:S(2)}) collective-permute-start(f32[1,8,64]{2,1,0:T(8,128)S(1)} %broadcast.62), channel_id=1, source_target_pairs={{32,0},{64,32},{96,64},{128,96},{160,128},{192,160},{224,192},{33,... | collective-permute-start | bytes 6152 | tf_op jit(solution)/shard_map/ppermute | solution.py:18
  116.8 24.5 %collective-permute-start.22 = (f32[18,18,1]{2,1,0:T(8,128)S(1)}, f32[18,18,1]{2,1,0:T(8,128)S(1)}, u32[]{:S(2)}, u32[]{:S(2)}) collective-permute-start(f32[18,18,1]{2,1,0:T(8,128)S(1)} %get-tuple-element.65), channel_id=1, source_target_pairs={{1,0},{2,1},{3,2},{5,4},{6,5},{7,6},{9,8},{10,9},{11,10},{13,12},{... | collective-permute-start | bytes 3896 | tf_op jit(solution)/shard_map/ppermute | solution.py:18
  118.1 24.5 %collective-permute-start.23 = (f32[18,18,1]{2,1,0:T(8,128)S(1)}, f32[18,18,1]{2,1,0:T(8,128)S(1)}, u32[]{:S(2)}, u32[]{:S(2)}) collective-permute-start(f32[18,18,1]{2,1,0:T(8,128)S(1)} %get-tuple-element.66), channel_id=1, source_target_pairs={{0,1},{1,2},{2,3},{4,5},{5,6},{6,7},{8,9},{9,10},{10,11},{12,13},{... | collective-permute-start | bytes 3896 | tf_op jit(solution)/shard_map/ppermute | solution.py:15
  122.9 34.1 %collective-permute-start.38 = (f32[1,8,64]{2,1,0:T(8,128)S(1)}, f32[1,8,64]{2,1,0:T(8,128)S(1)}, u32[]{:S(2)}, u32[]{:S(2)}) collective-permute-start(f32[1,8,64]{2,1,0:T(8,128)S(1)} %get-tuple-element.173), channel_id=1, source_target_pairs={{0,32},{32,64},{64,96},{96,128},{128,160},{160,192},{192,224},{1,3... | collective-permute-start | bytes 6152 | tf_op jit(solution)/shard_map/ppermute | solution.py:15
  141.3 17.6 collective-permute-start.36
  142.9 8.4 collective-permute-start.25
  148.6 17.5 collective-permute-start.43
  151.4 18.9 collective-permute-start.41
  153.3 9.3 collective-permute-start.27
  157.0 7.5 collective-permute-start.26
  158.9 31.5 %collective-permute-start.42 = (f32[10,1,64]{2,1,0:T(1,128)S(1)}, f32[10,1,64]{2,1,0:T(1,128)S(1)}, u32[]{:S(2)}, u32[]{:S(2)}) collective-permute-start(f32[10,1,64]{2,1,0:T(1,128)S(1)} %get-tuple-element.153), channel_id=1, source_target_pairs={{0,4},{4,8},{8,12},{12,16},{16,20},{20,24},{24,28},{1,5},{5,9},{9,... | collective-permute-start | bytes 7688 | tf_op jit(solution)/shard_map/ppermute | solution.py:15
  162.6 29.8 %collective-permute-start.40 = (f32[10,1,64]{2,1,0:T(1,128)S(1)}, f32[10,1,64]{2,1,0:T(1,128)S(1)}, u32[]{:S(2)}, u32[]{:S(2)}) collective-permute-start(f32[10,1,64]{2,1,0:T(1,128)S(1)} %get-tuple-element.154), channel_id=1, source_target_pairs={{4,0},{8,4},{12,8},{16,12},{20,16},{24,20},{28,24},{5,1},{9,5},{13... | collective-permute-start | bytes 7688 | tf_op jit(solution)/shard_map/ppermute | solution.py:18
  164.7 7.7 collective-permute-start.28
  166.0 8.1 collective-permute-start.29
  174.4 7.0 collective-permute-start.31
  178.7 7.1 collective-permute-start.30
  180.1 40.0 %collective-permute-start.45 = (f32[10,10,1]{2,1,0:T(8,128)S(1)}, f32[10,10,1]{2,1,0:T(8,128)S(1)}, u32[]{:S(2)}, u32[]{:S(2)}) collective-permute-start(f32[10,10,1]{2,1,0:T(8,128)S(1)} %get-tuple-element.135), channel_id=1, source_target_pairs={{1,0},{2,1},{3,2},{5,4},{6,5},{7,6},{9,8},{10,9},{11,10},{13,12},{... | collective-permute-start | bytes 1208 | tf_op jit(solution)/shard_map/ppermute | solution.py:18
  181.4 38.7 %collective-permute-start.47 = (f32[10,10,1]{2,1,0:T(8,128)S(1)}, f32[10,10,1]{2,1,0:T(8,128)S(1)}, u32[]{:S(2)}, u32[]{:S(2)}) collective-permute-start(f32[10,10,1]{2,1,0:T(8,128)S(1)} %get-tuple-element.136), channel_id=1, source_target_pairs={{0,1},{1,2},{2,3},{4,5},{5,6},{6,7},{8,9},{9,10},{10,11},{12,13},{... | collective-permute-start | bytes 1208 | tf_op jit(solution)/shard_map/ppermute | solution.py:15
  195.6 9.1 collective-permute-start.34
  196.9 9.2 collective-permute-start.35
  201.3 18.8 collective-permute-start.46
  204.7 15.4 collective-permute-start.44
  285.0 7.1 collective-permute-start.63
  301.6 10.9 collective-permute-start.67
  305.2 7.2 collective-permute-start.66
  306.5 20.6 %collective-permute-start.72 = (f32[1,4,32]{2,1,0:T(4,128)S(1)}, f32[1,4,32]{2,1,0:T(4,128)S(1)}, u32[]{:S(2)}, u32[]{:S(2)}) collective-permute-start(f32[1,4,32]{2,1,0:T(4,128)S(1)} %get-tuple-element.225), channel_id=1, source_target_pairs={{32,0},{64,32},{96,64},{128,96},{160,128},{192,160},{224,192},{33,... | collective-permute-start | bytes 1544 | tf_op jit(solution)/shard_map/ppermute | solution.py:18
  307.8 19.3 %collective-permute-start.74 = (f32[1,4,32]{2,1,0:T(4,128)S(1)}, f32[1,4,32]{2,1,0:T(4,128)S(1)}, u32[]{:S(2)}, u32[]{:S(2)}) collective-permute-start(f32[1,4,32]{2,1,0:T(4,128)S(1)} %get-tuple-element.226), channel_id=1, source_target_pairs={{0,32},{32,64},{64,96},{96,128},{128,160},{160,192},{192,224},{1,3... | collective-permute-start | bytes 1544 | tf_op jit(solution)/shard_map/ppermute | solution.py:15
  312.5 6.8 collective-permute-start.69
  321.2 10.3 collective-permute-start.70
  322.5 9.0 collective-permute-start.71
  327.2 10.7 collective-permute-start.78
  329.4 8.5 collective-permute-start.76
  340.9 11.8 collective-permute-start.79
  345.8 7.0 collective-permute-start.77
  347.8 11.3 collective-permute-start.82
  351.5 7.6 collective-permute-start.80
  522.8 7.0 collective-permute-start.87
  1788.0 8.1 collective-permute-start.154
  1789.3 8.5 collective-permute-start.155
  1805.4 7.6 collective-permute-start.159
  1816.2 8.1 collective-permute-start.160
  1817.5 8.5 collective-permute-start.161
  1833.6 6.8 collective-permute-start.165
  1843.6 8.1 collective-permute-start.166
  1844.9 8.5 collective-permute-start.167
  1869.4 8.1 collective-permute-start.172
  1870.7 8.5 collective-permute-start.173
  1895.3 8.1 collective-permute-start.178
  1896.6 8.5 collective-permute-start.179
  (120 other events, 789.7 us)
where the time goes:
time: 1920 us; the launch traced here: 1910 us
  blocking collectives  1110 us (58%)
  starting transfers between devices  509 us (27%)
  waiting for transfers between devices  191 us (10%)
  local copies, waits for them, and re-layouts  39.7 us (2%)
  other arithmetic  30.8 us (2%)
  between operations  24.2 us (1%)
    psum x8, blocking collectives, global_norm(): return lax.psum(jnp.sum(values * values), ('gx', 'gy', 'gz'))  587 us
    psum x7, blocking collectives, global_curvature(): return lax.psum(jnp.sum(direction * image), ('gx', 'gy', 'gz'))  525 us
    ppermute x90, starting transfers between devices, with_halo(): lax.ppermute(lax.slice_in_dim(block, block.shape[dim] - width, None, axis...  374 us
    ppermute x90, waiting for transfers between devices, with_halo(): lax.ppermute(lax.slice_in_dim(block, 0, width, axis=dim), axis, backward)  161 us
    ppermute x90, starting transfers between devices, with_halo(): lax.ppermute(lax.slice_in_dim(block, 0, width, axis=dim), axis, backward)  135 us
  transfers between devices with their start and end apart: 180, of which 77 were waited for; matrix products, arithmetic and copies ran while one was open for 3% of the time, Pallas kernels for 0%

commit v1 on v0

v1 whole, which is shorter than its diff:
```python
import itertools

import jax
import jax.numpy as jnp
from jax import lax
from jax.experimental import pallas as pl
from jax.experimental.pallas import tpu as pltpu
from jax.sharding import PartitionSpec as P

CG_ITERS = 8
MESH = pl.DeviceIdType.MESH
AXES = ("gx", "gy", "gz")
SIZES = (8, 8, 4)
F32 = jnp.float32
BF16 = jnp.bfloat16

ALL26 = [o for o in itertools.product((-1, 0, 1), repeat=3) if o != (0, 0, 0)]
XY8 = [o for o in ALL26 if o[2] == 0]
Z18 = [o for o in ALL26 if o[2] != 0]
Z2 = [(0, 0, -1), (0, 0, 1)]
RING7 = [(k, 0, 0) for k in range(1, 8)]
PLANE31 = [(0, j, k) for j in range(8) for k in range(4) if (j, k) != (0, 0)]


def canonical(offset):
    return tuple(o % n for o, n in zip(offset, SIZES))


PARTNERS = sorted({canonical(o) for o in ALL26 + RING7 + PLANE31})


def source_span(d, start, count, halo):
    if d == 0:
        return pl.ds(start, count)
    return pl.ds(start + count - halo, halo) if d > 0 else pl.ds(start, halo)


def target_span(d, start, count, halo):
    if d == 0:
        return pl.ds(start, count)
    return pl.ds(start - halo, halo) if d > 0 else pl.ds(start + count, halo)


def iota(shape, dim):
    return lax.broadcasted_iota(jnp.int32, shape, dim)


def pick(values, matrix):
    high = values.astype(BF16)
    rest = values - high.astype(F32)
    middle = rest.astype(BF16)
    low = (rest - middle.astype(F32)).astype(BF16)
    out = jnp.dot(low, matrix, preferred_element_type=F32)
    out = out + jnp.dot(middle, matrix, preferred_element_type=F32)
    return out + jnp.dot(high, matrix, preferred_element_type=F32)


def roll(value, shift):
    shift = shift % 128
    return value if shift == 0 else pltpu.roll(value, shift, 1)


def kernel(f_in, u_in, s_in, b_in, x_out, r_out, E0, M0, ZR0, V0, PB0, A0, D0, DG0, FD0,
           C1, R1s, RZ1, S1, M1, ZR1, PS, V1, PB1, A1, D1, DG1, FD1,
           EU, MU, ZU, T16, T8, T4, X16, XB, GC, GS, S2, B2, A2, DG2, PD, RM, AP, XL,
           sem_in, s_e0, r_e0, s_c1z, r_c1z, s_c1, r_c1, s_e2, r_e2, s_uz, r_uz, s_u, r_u,
           s_ps, r_ps, s_gc1, r_gc1, s_gc2, r_gc2, s_gs1, r_gs1, s_gs2, r_gs2):
    gx, gy, gz = (lax.axis_index(a) for a in AXES)
    me = (gx, gy, gz)

    def device(offset):
        return tuple(lax.rem(m + (o % n), n) if o % n else m for m, o, n in zip(me, offset, SIZES))

    def send(src, dst, ssem, rsem, offset):
        copy = pltpu.make_async_remote_copy(src_ref=src, dst_ref=dst, send_sem=ssem, recv_sem=rsem,
                                            device_id=device(offset), device_id_type=MESH)
        copy.start()
        return copy

    def wait(copies):
        for copy in copies:
            copy.wait()

    local = [pltpu.make_async_copy(src, E0.at[k, pl.ds(6, 16), pl.ds(8, 16)], sem_in.at[k])
             for k, src in enumerate((f_in, s_in, u_in, b_in))]
    for copy in local:
        copy.start()
    barrier = pltpu.get_barrier_semaphore()
    for offset in PARTNERS:
        pl.semaphore_signal(barrier, inc=1, device_id=device(offset), device_id_type=MESH)

    q24 = (iota((24, 128), 0) + iota((24, 128), 1)) % 2 == 1
    q32 = (iota((32, 128), 0) + iota((32, 128), 1)) % 2 == 1
    q16 = (iota((16, 128), 0) + iota((16, 128), 1)) % 2 == 1
    lane24 = iota((24, 128), 1)
    one, zero = jnp.float32(1.0), jnp.float32(0.0)

    def y_mask(rows, own_start, own_count):
        row = iota((rows, 128), 0)
        low = jnp.where(gy == 0, zero, one)
        high = jnp.where(gy == 7, zero, one)
        return jnp.where(row < own_start, low, jnp.where(row >= own_start + own_count, high, one))

    def z_mask(rows, low_at, high_at):
        lane = iota((rows, 128), 1)
        low = jnp.where(gz == 0, zero, one)
        high = jnp.where(gz == 3, zero, one)
        return jnp.where(low_at(lane), low, jnp.where(high_at(lane), high, one))

    y32 = y_mask(32, 8, 16)
    mask0 = (y32, y32 * z_mask(32, lambda l: l >= 64, lambda l: l < 64))
    mask1 = (y_mask(40, 16, 8) * z_mask(40, lambda l: l < 32, lambda l: l >= 96),)

    def x_scalar(p, low_end, high_start):
        outside = ((gx == 0) & (p < low_end)) | ((gx == 7) & (p >= high_start))
        return jnp.where(outside, zero, one)

    PD[...] = jnp.zeros_like(PD)
    B2[...] = jnp.zeros_like(B2)
    V1[...] = jnp.zeros_like(V1)
    PB1[...] = jnp.zeros_like(PB1)

    row, col = iota((128, 128), 0), iota((128, 128), 1)
    to_one = jnp.where((col >= 32) & (col < 96) & (col - 32 == row // 2), 0.125, 0.0).astype(BF16)
    to_two = jnp.where((row >= 32) & (row < 96) & (col == (row - 32) // 2), 0.125, 0.0).astype(BF16)
    from_two = jnp.where((col - 32 + 64 * gz + 128) // 2 - 64 == row, 1.0, 0.0).astype(BF16)
    from_one = jnp.where(row - 32 == col // 2, 1.0, 0.0).astype(BF16)
    from_one_edge = jnp.where(
        ((col < 64) & (row == 96 + col // 2)) | ((col >= 64) & (row == col // 2 - 32)), 1.0, 0.0
    ).astype(BF16)

    def restrict_one(sums):
        T16[...] = sums
        folded = T16[:, pl.ds(0, 8, stride=2), :] + T16[:, pl.ds(1, 8, stride=2), :]
        return pick(folded.reshape(64, 128), to_one).reshape(8, 8, 128)

    def restrict_two(sums):
        T8[...] = sums
        total = None
        for x in range(4):
            folded = T8[x, pl.ds(0, 4, stride=2), :] + T8[x, pl.ds(1, 4, stride=2), :]
            T4[x, 0:4] = folded
        full = pick(T4[...].reshape(32, 128), to_two).reshape(4, 8, 128)
        for x in range(4):
            term = roll(full[x], 32 * x)
            total = term if total is None else total + term
        return total[0:4]

    for copy in local:
        copy.wait()

    lane16 = iota((16, 128), 1)
    group = lane16 // 16

    def pack_rows(k, carry):
        total = jnp.zeros((16, 128), F32)
        for odd in range(2):
            for a in range(4):
                value = E0[a, 6 + 2 * k + odd, pl.ds(8, 16), :]
                total = jnp.where(group == 4 * odd + a, roll(value, 8 + 16 * a + 64 * odd), total)
        M0[k] = total
        return carry

    lax.fori_loop(0, 8, pack_rows, 0)
    pl.semaphore_wait(barrier, len(PARTNERS))

    e0 = []
    for n, (dx, dy, dz) in enumerate(ALL26):
        if dz == 0:
            hx = 4 if dx and dy else 5
            e0.append(send(E0.at[:, source_span(dx, 6, 16, hx), source_span(dy, 8, 16, 8)],
                           E0.at[:, target_span(dx, 6, 16, hx), target_span(dy, 8, 16, 8)],
                           s_e0.at[n], r_e0.at[n], (dx, dy, dz)))
        else:
            side = 0 if dz > 0 else 1
            e0.append(send(M0.at[source_span(dx, 0, 8, 2), source_span(dy, 0, 16, 8)],
                           ZR0.at[side, target_span(dx, 2, 8, 2), target_span(dy, 8, 16, 8)],
                           s_e0.at[n], r_e0.at[n], (dx, dy, dz)))

    for k, a in ((0, 1), (1, 3)):
        sums = jnp.stack([E0[a, 6 + 2 * x, pl.ds(8, 16), :] + E0[a, 7 + 2 * x, pl.ds(8, 16), :] for x in range(8)])
        C1[k, pl.ds(8, 8), pl.ds(8, 8)] = restrict_one(sums)
        for x in range(8):
            R1s[k, x] = roll(C1[k, 8 + x, pl.ds(8, 8), :], 64)
    c1z = [send(R1s, RZ1.at[n], s_c1z.at[n], r_c1z.at[n], (0, 0, 1 if n == 0 else -1)) for n in range(2)]
    mine = gy * 4 + gz
    for k in range(2):
        sums = jnp.stack([C1[k, 8 + 2 * x, pl.ds(8, 8), :] + C1[k, 9 + 2 * x, pl.ds(8, 8), :] for x in range(4)])
        GC[mine, gx, k] = restrict_two(sums)
    gc1 = [send(GC.at[mine, gx], GC.at[mine, gx], s_gc1.at[n], r_gc1.at[n], o) for n, o in enumerate(RING7)]
    wait(c1z)
    lane8 = iota((8, 128), 1)
    for k in range(2):
        for x in range(8):
            own = C1[k, 8 + x, pl.ds(8, 8), :]
            C1[k, 8 + x, pl.ds(8, 8), :] = jnp.where(
                lane8 < 32, RZ1[0, k, x], jnp.where(lane8 < 96, own, RZ1[1, k, x]))
    c1 = [send(C1.at[:, source_span(dx, 8, 8, 8), source_span(dy, 8, 8, 8)],
               C1.at[:, target_span(dx, 8, 8, 8), target_span(dy, 8, 8, 8)],
               s_c1.at[n], r_c1.at[n], (dx, dy, 0)) for n, (dx, dy, _) in enumerate(XY8)]

    def around(O, tiles, c, i, r0, q):
        out = []
        centre = [O[t, 1 - c, i + 1, pl.ds(r0, 24), :] for t in range(tiles)]
        ups = [roll(v, -1) for v in centre]
        downs = [roll(v, 1) for v in centre]
        for t in range(tiles):
            low = O[t, 1 - c, i, pl.ds(r0, 24), :]
            high = O[t, 1 - c, i + 2, pl.ds(r0, 24), :]
            other = jnp.where(q, high, low) if c == 0 else jnp.where(q, low, high)
            yp = O[t, 1 - c, i + 1, pl.ds(r0 + 1, 24), :]
            ym = O[t, 1 - c, i + 1, pl.ds(r0 - 1, 24), :]
            if tiles == 2:
                zp = jnp.where(lane24 == 127, ups[1 - t], ups[t])
                zm = jnp.where(lane24 == 0, downs[1 - t], downs[t])
            else:
                zp, zm = ups[0], downs[0]
            out.append((centre[t], other, yp, ym, zp, zm))
        return out

    def coefficients(PB, A, D, DG, tiles, r0, scale, shift_of, mask, x_of):
        for c in range(2):
            def body(i, carry):
                near = around(PB, tiles, c, i, r0, q24)
                for t in range(tiles):
                    b = PB[t, c, i + 1, pl.ds(r0, 24), :]
                    total = shift_of(t, c, i)
                    weights = [(0.5 * scale) * (b + v) for v in near[t]]
                    for w in weights:
                        total = total + w
                    inverse = (1.0 / total) * (mask[t][r0:r0 + 24] * x_of(i + 1))
                    DG[t, c, i] = total
                    D[t, c, i] = inverse
                    for k, w in enumerate(weights):
                        A[t, c, k, i] = w * inverse
                return carry
            lax.fori_loop(0, 12, body, 0)

    def relaxed(V, A, FD, tiles, c, i, r0):
        near = around(V, tiles, c, i, r0, q24)
        out = []
        for t in range(tiles):
            total = FD[t, c, i]
            for k, v in enumerate(near[t]):
                total = total + A[t, c, k, i] * v
            out.append(total)
        return out

    def half(V, A, FD, tiles, c, r0, lo, hi):
        def body(i, carry):
            new = relaxed(V, A, FD, tiles, c, i, r0)
            for t in range(tiles):
                V[t, c, i + 1, pl.ds(r0, 24), :] = new[t]
            return carry
        lax.fori_loop(lo, hi, body, 0)

    def sweeps(V, A, FD, tiles, r0, lo=0, hi=12, first=0):
        for step in range(first, 4):
            half(V, A, FD, tiles, step % 2, r0, lo, hi)

    def residual_pair(V, A, FD, DG, tiles, i, r0):
        out = []
        for c in range(2):
            new = relaxed(V, A, FD, tiles, c, i, r0)[0]
            out.append(DG[0, c, i] * (new - V[0, c, i + 1, pl.ds(r0, 24), :]))
        return out

    def unpack(red, black, q):
        return jnp.where(q, black, red), jnp.where(q, red, black)

    wait(e0)

    lane32 = iota((32, 128), 1)

    def edge_of(a, p):
        merged = jnp.where(lane32 % 16 < 8, ZR0[0, p - 1], ZR0[1, p - 1])
        return roll(merged, -(16 * a + 8)), roll(merged, -(16 * a + 72))

    x0 = lambda p: x_scalar(p, 3, 11)
    x1 = lambda p: x_scalar(p, 5, 9)

    def pack0(p, carry):
        xs = x0(p)
        for dst, a in ((V0, 2), (PB0, 3)):
            even, odd = E0[a, 2 * p], E0[a, 2 * p + 1]
            m = mask0[0] * xs
            dst[0, 0, p] = jnp.where(q32, odd, even) * m
            dst[0, 1, p] = jnp.where(q32, even, odd) * m
        return carry

    lax.fori_loop(0, 14, pack0, 0)
    for p in (0, 13):
        for dst in (V0, PB0):
            for c in range(2):
                dst[1, c, p] = jnp.zeros((32, 128), F32)

    def pack0_edge(p, carry):
        xs = x0(p)
        for dst, a in ((V0, 2), (PB0, 3)):
            even, odd = edge_of(a, p)
            m = mask0[1] * xs
            dst[1, 0, p] = jnp.where(q32, odd, even) * m
            dst[1, 1, p] = jnp.where(q32, even, odd) * m
        for dst, a in ((FD0, 0), (DG0, 1)):
            even, odd = edge_of(a, p)
            dst[1, 0, p - 1] = jnp.where(q32, odd, even)[4:28]
            dst[1, 1, p - 1] = jnp.where(q32, even, odd)[4:28]
            even, odd = E0[a, 2 * p, pl.ds(4, 24), :], E0[a, 2 * p + 1, pl.ds(4, 24), :]
            dst[0, 0, p - 1] = jnp.where(q24, odd, even)
            dst[0, 1, p - 1] = jnp.where(q24, even, odd)
        return carry

    lax.fori_loop(1, 13, pack0_edge, 0)
    coefficients(PB0, A0, D0, DG0, 2, 4, 1.0, lambda t, c, i: DG0[t, c, i], mask0, x0)

    def scale_rhs0(i, carry):
        for t in range(2):
            for c in range(2):
                FD0[t, c, i] = FD0[t, c, i] * D0[t, c, i]
        return carry

    lax.fori_loop(0, 12, scale_rhs0, 0)
    sweeps(V0, A0, FD0, 2, 4)

    sums = []
    for i in range(2, 10):
        red, black = residual_pair(V0, A0, FD0, DG0, 2, i, 4)
        sums.append((red + black)[4:20])
    S1[pl.ds(8, 8), pl.ds(8, 8)] = restrict_one(jnp.stack(sums))
    slot = iota((8, 128), 1) // 16
    for g in range(2):
        total = jnp.zeros((8, 128), F32)
        for k in range(4):
            value = roll(S1[8 + 4 * g + k, pl.ds(8, 8), :], 64 + 32 * k)
            total = jnp.where((slot == 1 + 2 * k) | (slot == (6 + 2 * k) % 8), value, total)
        M1[g] = total
    e2 = []
    for n, (dx, dy, dz) in enumerate(ALL26):
        if dz == 0:
            e2.append(send(S1.at[source_span(dx, 8, 8, 4), source_span(dy, 8, 8, 8)],
                           S1.at[target_span(dx, 8, 8, 4), target_span(dy, 8, 8, 8)],
                           s_e2.at[n], r_e2.at[n], (dx, dy, dz)))
        else:
            side = 0 if dz > 0 else 1
            e2.append(send(M1.at[source_span(dx, 0, 2, 1), source_span(dy, 0, 8, 8)],
                           ZR1.at[side, target_span(dx, 1, 2, 1), target_span(dy, 8, 8, 8)],
                           s_e2.at[n], r_e2.at[n], (dx, dy, dz)))

    wait(gc1)
    gc2 = [send(GC.at[mine], GC.at[mine], s_gc2.at[n], r_gc2.at[n], o) for n, o in enumerate(PLANE31)]
    for i in range(2, 10):
        red, black = V0[0, 0, i + 1, pl.ds(8, 16), :], V0[0, 1, i + 1, pl.ds(8, 16), :]
        EU[0, 2 * i + 2, pl.ds(8, 16)], EU[0, 2 * i + 3, pl.ds(8, 16)] = unpack(red, black, q16)
    for g in range(2):
        total = jnp.zeros((16, 128), F32)
        for k in range(8):
            total = jnp.where(group == k, roll(EU[0, 6 + 8 * g + k, pl.ds(8, 16), :], 8 + 16 * k), total)
        MU[g] = total
    uz = [send(MU, ZU.at[n], s_uz.at[n], r_uz.at[n], (0, 0, 1 if n == 0 else -1)) for n in range(2)]

    wait(c1)

    def pack1(p, carry):
        xs = x1(p)
        m = mask1[0][8:32] * xs
        even, odd = C1[1, 2 * p - 2], C1[1, 2 * p - 1]
        PB1[0, 0, p, pl.ds(8, 24), :] = jnp.where(q24, odd, even) * m
        PB1[0, 1, p, pl.ds(8, 24), :] = jnp.where(q24, even, odd) * m
        even, odd = C1[0, 2 * p - 2], C1[0, 2 * p - 1]
        DG1[0, 0, p - 1] = jnp.where(q24, odd, even)
        DG1[0, 1, p - 1] = jnp.where(q24, even, odd)
        return carry

    lax.fori_loop(1, 13, pack1, 0)
    coefficients(PB1, A1, D1, DG1, 1, 8, 0.25, lambda t, c, i: DG1[t, c, i], mask1, x1)

    wait(e2)
    slot24 = lane24 // 16
    for x in range(4, 20):
        g = (x - 4) // 4
        merged = jnp.where(slot24 % 2 == 1, ZR1[0, g], ZR1[1, g])
        halo = roll(merged, -32 * (x % 4))
        S1[x] = jnp.where((lane24 >= 32) & (lane24 < 96), S1[x], halo)
    PS[1, pl.ds(8, 8), pl.ds(8, 8)] = S1[pl.ds(8, 8), pl.ds(8, 8)]

    def rhs1(source, lo, hi):
        def body(i, carry):
            even, odd = source[2 * i], source[2 * i + 1]
            FD1[0, 0, i] = jnp.where(q24, odd, even) * D1[0, 0, i]
            FD1[0, 1, i] = jnp.where(q24, even, odd) * D1[0, 1, i]
            return carry
        lax.fori_loop(lo, hi, body, 0)

    rhs1(S1, 2, 10)
    for i in range(2, 10):
        V1[0, 0, i + 1, pl.ds(8, 24), :] = FD1[0, 0, i]
    sweeps(V1, A1, FD1, 1, 8, 2, 10, first=1)
    sums = []
    for i in range(4, 8):
        red, black = residual_pair(V1, A1, FD1, DG1, 1, i, 8)
        sums.append((red + black)[8:16])
    GS[mine, gx] = restrict_two(jnp.stack(sums))
    gs1 = [send(GS.at[mine, gx], GS.at[mine, gx], s_gs1.at[n], r_gs1.at[n], o) for n, o in enumerate(RING7)]

    q8 = (iota((8, 128), 0) + iota((8, 128), 1)) % 2 == 1
    for i in range(4, 8):
        red, black = V1[0, 0, i + 1, pl.ds(16, 8), :], V1[0, 1, i + 1, pl.ds(16, 8), :]
        PS[0, 2 * i, pl.ds(8, 8)], PS[0, 2 * i + 1, pl.ds(8, 8)] = unpack(red, black, q8)
    ps = [send(PS.at[:, source_span(dx, 8, 8, 8), source_span(dy, 8, 8, 8)],
               PS.at[:, target_span(dx, 8, 8, 8), target_span(dy, 8, 8, 8)],
               s_ps.at[n], r_ps.at[n], (dx, dy, 0)) for n, (dx, dy, _) in enumerate(XY8)]
    wait(uz)
    for x in range(16):
        merged = jnp.where(lane16 % 16 < 8, ZU[0, x // 8], ZU[1, x // 8])
        EU[1, 6 + x, pl.ds(8, 16)] = roll(merged, -(16 * (x % 8) + 8))
    wait(gs1)
    gs2 = [send(GS.at[mine], GS.at[mine], s_gs2.at[n], r_gs2.at[n], o) for n, o in enumerate(PLANE31)]
    eu = [send(EU.at[:, source_span(dx, 6, 16, 5), source_span(dy, 8, 16, 8)],
               EU.at[:, target_span(dx, 6, 16, 5), target_span(dy, 8, 16, 8)],
               s_u.at[n], r_u.at[n], (dx, dy, 0)) for n, (dx, dy, _) in enumerate(XY8)]

    lane_group = lane8 // 32

    def spread(load, store):
        def body(g, carry):
            for pair in range(4):
                blocks = [jnp.concatenate([load(8 * pair + k, g), load(8 * pair + 4 + k, g)], axis=0)
                          for k in range(4)]
                for x in range(4):
                    total = roll(blocks[0], -32 * x)
                    for k in range(1, 4):
                        total = jnp.where(lane_group == k, roll(blocks[k], 32 * (k - x)), total)
                    store(4 * g + x, 8 * pair, total)
            return carry
        lax.fori_loop(0, 8, body, 0)

    def store_s2(x, y, v):
        S2[x, pl.ds(y, 8), :] = v

    def store_b2(x, y, v):
        B2[x + 4, pl.ds(y + 8, 8), :] = v

    def store_source(x, y, v):
        PD[x + 4, pl.ds(y + 8, 8), :] = v
        RM[x, pl.ds(y, 8), :] = v

    wait(gc2)
    spread(lambda j, g: GC[j, g, 0], store_s2)
    spread(lambda j, g: GC[j, g, 1], store_b2)

    def shifts(O, x):
        centre = O[x + 4, pl.ds(8, 32), :]
        return (centre, (O[x + 5, pl.ds(8, 32), :], O[x + 3, pl.ds(8, 32), :], O[x + 4, pl.ds(9, 32), :],
                         O[x + 4, pl.ds(7, 32), :], roll(centre, -1), roll(centre, 1)))

    def weights2(x, carry):
        b, near = shifts(B2, x)
        total = S2[x]
        for k, v in enumerate(near):
            if k == 4:
                v = jnp.where(lane32 == 127, 0.0, v)
            if k == 5:
                v = jnp.where(lane32 == 0, 0.0, v)
            w = (0.5 * 0.0625) * (b + v)
            total = total + w
            if k == 4:
                w = jnp.where(lane32 == 127, 0.0, w)
            if k == 5:
                w = jnp.where(lane32 == 0, 0.0, w)
            A2[k, x] = w
        DG2[x] = total
        return carry

    lax.fori_loop(0, 32, weights2, 0)

    wait(ps)

    def pack1_post(p, carry):
        m = mask1[0][8:32] * x1(p)
        even, odd = PS[0, 2 * p - 2], PS[0, 2 * p - 1]
        V1[0, 0, p, pl.ds(8, 24), :] = jnp.where(q24, odd, even) * m
        V1[0, 1, p, pl.ds(8, 24), :] = jnp.where(q24, even, odd) * m
        return carry

    lax.fori_loop(1, 13, pack1_post, 0)
    rhs1(PS.at[1], 0, 12)

    wait(eu)

    def pack0_post(p, carry):
        xs = x0(p)
        for t in range(2):
            m = mask0[t] * xs
            even, odd = EU[t, 2 * p], EU[t, 2 * p + 1]
            V0[t, 0, p] = jnp.where(q32, odd, even) * m
            V0[t, 1, p] = jnp.where(q32, even, odd) * m
        return carry

    lax.fori_loop(0, 14, pack0_post, 0)

    wait(gs2)
    spread(lambda j, g: GS[j, g], store_source)
    XL[...] = jnp.zeros_like(XL)

    def whole(total):
        return jnp.sum(jnp.sum(total, axis=0, keepdims=True), axis=1, keepdims=True)

    def square(x, total):
        return total + RM[x] * RM[x]

    acc = jnp.zeros((32, 128), F32)
    rr = whole(lax.fori_loop(0, 32, square, acc))
    for step in range(CG_ITERS):
        def image(x, total):
            p, near = shifts(PD, x)
            value = DG2[x] * p
            for k, v in enumerate(near):
                value = value - A2[k, x] * v
            AP[x] = value
            return total + p * value

        alpha = rr / whole(lax.fori_loop(0, 32, image, acc))

        def gain(x, carry):
            XL[x] = XL[x] + alpha * PD[4 * gx + x, pl.ds(4 * gy + 4, 16), :]
            return carry

        lax.fori_loop(0, 12, gain, 0)
        if step < CG_ITERS - 1:
            def update(x, total):
                value = RM[x] - alpha * AP[x]
                RM[x] = value
                return total + value * value

            new = whole(lax.fori_loop(0, 32, update, acc))
            ratio = new / rr

            def turn(x, carry):
                PD[x + 4, pl.ds(8, 32), :] = RM[x] + ratio * PD[x + 4, pl.ds(8, 32), :]
                return carry

            lax.fori_loop(0, 32, turn, 0)
            rr = new

    fine = pick(XL[...].reshape(192, 128), from_two).reshape(12, 16, 128)
    X16[:, pl.ds(0, 16, stride=2), :] = fine
    X16[:, pl.ds(1, 16, stride=2), :] = fine

    def correct1(i, carry):
        for c in range(2):
            V1[0, c, i + 1, pl.ds(8, 24), :] = V1[0, c, i + 1, pl.ds(8, 24), :] + X16[i, 0:24]
        return carry

    lax.fori_loop(0, 12, correct1, 0)
    sweeps(V1, A1, FD1, 1, 8)

    planes = []
    for p in range(14):
        k = (p + 7) // 2
        red, black = V1[0, 0, k, pl.ds(12, 16), :], V1[0, 1, k, pl.ds(12, 16), :]
        planes.append(unpack(red, black, q16)[0 if p % 2 else 1])
    coarse = jnp.stack(planes).reshape(224, 128)
    for t, matrix in enumerate((from_one, from_one_edge)):
        fine = pick(coarse, matrix).reshape(14, 16, 128)
        XB[:, pl.ds(0, 16, stride=2), :] = fine
        XB[:, pl.ds(1, 16, stride=2), :] = fine

        def correct0(p, carry):
            for c in range(2):
                V0[t, c, p] = V0[t, c, p] + XB[p]
            return carry

        lax.fori_loop(0, 14, correct0, 0)
    sweeps(V0, A0, FD0, 2, 4)

    def finish(i, carry):
        red, black = residual_pair(V0, A0, FD0, DG0, 2, i, 4)
        even, odd = unpack(red, black, q24)
        r_out[2 * i - 4] = even[4:20]
        r_out[2 * i - 3] = odd[4:20]
        even, odd = unpack(V0[0, 0, i + 1, pl.ds(8, 16), :], V0[0, 1, i + 1, pl.ds(8, 16), :], q16)
        x_out[2 * i - 4] = even
        x_out[2 * i - 3] = odd
        return carry

    lax.fori_loop(2, 10, finish, 0)


def vmem(*shape):
    return pltpu.VMEM(shape, F32)


def dma(*shape):
    return pltpu.SemaphoreType.DMA(shape)


SCRATCH = [
    vmem(4, 28, 32, 128), vmem(8, 16, 128), vmem(2, 12, 32, 128),
    vmem(2, 2, 14, 32, 128), vmem(2, 2, 14, 32, 128), vmem(2, 2, 6, 12, 24, 128),
    vmem(2, 2, 12, 24, 128), vmem(2, 2, 12, 24, 128), vmem(2, 2, 12, 24, 128),
    vmem(2, 24, 24, 128), vmem(2, 8, 8, 128), vmem(2, 2, 8, 8, 128),
    vmem(24, 24, 128), vmem(2, 8, 128), vmem(2, 4, 24, 128), vmem(2, 24, 24, 128),
    vmem(1, 2, 14, 40, 128), vmem(1, 2, 14, 40, 128), vmem(1, 2, 6, 12, 24, 128),
    vmem(1, 2, 12, 24, 128), vmem(1, 2, 12, 24, 128), vmem(1, 2, 12, 24, 128),
    vmem(2, 28, 32, 128), vmem(2, 16, 128), vmem(2, 2, 16, 128),
    vmem(8, 16, 128), vmem(4, 8, 128), vmem(4, 8, 128), vmem(12, 32, 128), vmem(14, 32, 128),
    vmem(32, 8, 2, 4, 128), vmem(32, 8, 4, 128),
    vmem(32, 32, 128), vmem(40, 48, 128), vmem(6, 32, 32, 128), vmem(32, 32, 128),
    vmem(40, 48, 128), vmem(32, 32, 128), vmem(32, 32, 128), vmem(12, 16, 128),
    dma(4), dma(26), dma(26), dma(2), dma(2), dma(8), dma(8), dma(26), dma(26), dma(2), dma(2), dma(8), dma(8),
    dma(8), dma(8), dma(7), dma(7), dma(31), dma(31), dma(7), dma(7), dma(31), dma(31),
]


def solution(mesh):
    def local(right_side, initial, shift, beta):
        shape = jax.ShapeDtypeStruct(right_side.shape, F32)
        return pl.pallas_call(
            kernel,
            out_shape=(shape, shape),
            in_specs=[pl.BlockSpec(memory_space=pl.ANY)] * 4,
            out_specs=(pl.BlockSpec(memory_space=pltpu.VMEM),) * 2,
            scratch_shapes=SCRATCH,
            compiler_params=pltpu.CompilerParams(
                collective_id=0, has_side_effects=True, vmem_limit_bytes=56 * 2**20),
        )(right_side, initial, shift, beta)

    spec = P(*AXES)
    return jax.shard_map(local, mesh=mesh, in_specs=(spec,) * 4, out_specs=(spec, spec), check_vma=False)
```

time: 1920 us -> 102 us (0.05)
  blocking collectives: 1110 us -> 0 us
  starting transfers between devices: 509 us -> 0 us
  waiting for transfers between devices: 191 us -> 0 us
  Pallas kernels: 0 us -> 98.8 us
  local copies, waits for them, and re-layouts: 39.7 us -> 2.26 us
  other arithmetic: 30.8 us -> 0 us
  between operations: 24.2 us -> 0.65 us
    psum x15 -> x0, blocking collectives: 1110 us -> none  [the longest x8 587 us: global_norm(): return lax.psum(jnp.sum(values * values), ('gx', 'gy', 'gz'))]
    ppermute x180 -> x0, starting transfers between devices: 509 us -> none  [the longest x90 374 us: with_halo(): lax.ppermute(lax.slice_in_dim(block, block.shape[dim] - width, None, axis...]
    ppermute x180 -> x0, waiting for transfers between devices: 191 us -> none  [the longest x90 161 us: with_halo(): lax.ppermute(lax.slice_in_dim(block, 0, width, axis=dim), axis, backward)]
    pallas_call x0 -> x1, Pallas kernels: none -> 98.8 us  [local(): pl.pallas_call(kernel, out_shape=(shape, shape), in_specs=[pl.BlockSpec(m...]
    reshape x8 -> x0, local copies, waits for them, and re-layouts: 31.2 us -> none  [the longest x4 30.2 us: restrict(): values.reshape(size_a // 2, 2, size_b // 2, 2, size_c // 2, 2)]
    reduce_sum x21 -> x0, other arithmetic: 22.6 us -> none  [the longest x6 12.6 us: restrict(): values.reshape(size_a // 2, 2, size_b // 2, 2, size_c // 2, 2)]
  transfers between devices with their start and end apart: 180 -> 0, of which waited for: 77 -> 0; matrix products, arithmetic and copies ran while one was open for 3% -> 0% of each run, Pallas kernels for 0% -> 0%
where the time goes in v1:
time: 102 us
  Pallas kernels  98.8 us (97%)
  local copies, waits for them, and re-layouts  2.26 us (2%)
    pallas_call x1, Pallas kernels, local(): pl.pallas_call(kernel, out_shape=(shape, shape), in_specs=[pl.BlockSpec(m...  98.8 us
    unnamed x4, local copies, waits for them, and re-layouts  2.26 us

profile of v1, /device:TPU:1, one launch (start us, length us, event | category | flops | bytes accessed | tf_op | source)
XLA Modules:
  0.0 101.7 jit_solution(9924024212543726556)
XLA Ops:
  0.6 98.8 %shard_map.59 = (f32[16,16,128]{2,1,0:T(8,128)}, f32[16,16,128]{2,1,0:T(8,128)}) custom-call(f32[16,16,128]{2,1,0:T(8,128)} %f_in.1, f32[16,16,128]{2,1,0:T(8,128)} %u_in.1, f32[16,16,128]{2,1,0:T(8,128)} %s_in.1, f32[16,16,128]{2,1,0:T(8,128)} %b_in.1), custom_call_target="tpu_custom_call" | custom-call | tf_op jit(solution)/shard_map/pallas_call | solution.py:618
  99.4 0.0 copy-start
  99.5 1.6 %copy.8 = f32[16,16,128]{2,1,0:T(8,128)} copy(f32[16,16,128]{2,1,0:T(8,128)} %get-tuple-element.4) | data formatting | bytes 262144
  101.1 0.0 copy-done
  101.1 0.7 copy.9
Async XLA Ops:
  99.4 1.6 %copy-start = (f32[16,16,128]{2,1,0:T(8,128)S(1)}, f32[16,16,128]{2,1,0:T(8,128)}, u32[]{:S(2)}) copy-start(f32[16,16,128]{2,1,0:T(8,128)} %get-tuple-element.5) | copy-start | bytes 393220

commit v2 on v1

--- a/solution.py
+++ b/solution.py
@@ -16,17 +16,19 @@
 
 ALL26 = [o for o in itertools.product((-1, 0, 1), repeat=3) if o != (0, 0, 0)]
 XY8 = [o for o in ALL26 if o[2] == 0]
-Z18 = [o for o in ALL26 if o[2] != 0]
-Z2 = [(0, 0, -1), (0, 0, 1)]
+X6 = [o for o in XY8 if o[0] != 0]
 RING7 = [(k, 0, 0) for k in range(1, 8)]
-PLANE31 = [(0, j, k) for j in range(8) for k in range(4) if (j, k) != (0, 0)]
+ROW3 = [(0, 0, k) for k in range(1, 4)]
+CHIPS3 = [(0, j, 0) for j in (2, 4, 6)]
+SAME15 = sorted(((0, j, k) for j in (0, 2, 4, 6) for k in range(4) if (j, k) != (0, 0)),
+                key=lambda o: min(o[1], 8 - o[1]) // 2 + min(o[2], 4 - o[2]))
 
 
 def canonical(offset):
     return tuple(o % n for o, n in zip(offset, SIZES))
 
 
-PARTNERS = sorted({canonical(o) for o in ALL26 + RING7 + PLANE31})
+PARTNERS = sorted({canonical(o) for o in ALL26 + RING7 + [(0, 4, 0)]})
 
 
 def source_span(d, start, count, halo):
@@ -43,6 +45,15 @@
 
 def iota(shape, dim):
     return lax.broadcasted_iota(jnp.int32, shape, dim)
+
+
+def loop(lo, hi, body, init, unroll):
+    def chunk(k, carry):
+        for j in range(unroll):
+            carry = body(lo + k * unroll + j, carry)
+        return carry
+
+    return lax.fori_loop(0, (hi - lo) // unroll, chunk, init)
 
 
 def pick(values, matrix):
@@ -64,16 +75,20 @@
            C1, R1s, RZ1, S1, M1, ZR1, PS, V1, PB1, A1, D1, DG1, FD1,
            EU, MU, ZU, T16, T8, T4, X16, XB, GC, GS, S2, B2, A2, DG2, PD, RM, AP, XL,
            sem_in, s_e0, r_e0, s_c1z, r_c1z, s_c1, r_c1, s_e2, r_e2, s_uz, r_uz, s_u, r_u,
-           s_ps, r_ps, s_gc1, r_gc1, s_gc2, r_gc2, s_gs1, r_gs1, s_gs2, r_gs2):
+           s_ps, r_ps, s_gc1, r_gc1, s_gc2, r_gc2, s_gs1, r_gs1, s_gs2, r_gs2,
+           s_gc3, r_gc3, s_gc4, r_gc4, s_gs3, r_gs3, s_c1b, r_c1b):
     gx, gy, gz = (lax.axis_index(a) for a in AXES)
     me = (gx, gy, gz)
+    core = lax.rem(gy, 2)
+    twin = (gx, gy + 1 - 2 * core, gz)
 
     def device(offset):
         return tuple(lax.rem(m + (o % n), n) if o % n else m for m, o, n in zip(me, offset, SIZES))
 
-    def send(src, dst, ssem, rsem, offset):
+    def send(src, dst, ssem, rsem, offset=None):
         copy = pltpu.make_async_remote_copy(src_ref=src, dst_ref=dst, send_sem=ssem, recv_sem=rsem,
-                                            device_id=device(offset), device_id_type=MESH)
+                                            device_id=twin if offset is None else device(offset),
+                                            device_id_type=MESH)
         copy.start()
         return copy
 
@@ -114,11 +129,6 @@
     def x_scalar(p, low_end, high_start):
         outside = ((gx == 0) & (p < low_end)) | ((gx == 7) & (p >= high_start))
         return jnp.where(outside, zero, one)
-
-    PD[...] = jnp.zeros_like(PD)
-    B2[...] = jnp.zeros_like(B2)
-    V1[...] = jnp.zeros_like(V1)
-    PB1[...] = jnp.zeros_like(PB1)
 
     row, col = iota((128, 128), 0), iota((128, 128), 1)
     to_one = jnp.where((col >= 32) & (col < 96) & (col - 32 == row // 2), 0.125, 0.0).astype(BF16)
@@ -148,6 +158,14 @@
 
     for copy in local:
         copy.wait()
+    pl.semaphore_wait(barrier, len(PARTNERS))
+    e0 = []
+    for n, (dx, dy, dz) in enumerate(ALL26):
+        if dz == 0:
+            hx = 4 if dx and dy else 5
+            e0.append(send(E0.at[:, source_span(dx, 6, 16, hx), source_span(dy, 8, 16, 8)],
+                           E0.at[:, target_span(dx, 6, 16, hx), target_span(dy, 8, 16, 8)],
+                           s_e0.at[n], r_e0.at[n], (dx, dy, dz)))
 
     lane16 = iota((16, 128), 1)
     group = lane16 // 16
@@ -161,21 +179,18 @@
         M0[k] = total
         return carry
 
-    lax.fori_loop(0, 8, pack_rows, 0)
-    pl.semaphore_wait(barrier, len(PARTNERS))
-
-    e0 = []
+    loop(0, 8, pack_rows, 0, 4)
     for n, (dx, dy, dz) in enumerate(ALL26):
-        if dz == 0:
-            hx = 4 if dx and dy else 5
-            e0.append(send(E0.at[:, source_span(dx, 6, 16, hx), source_span(dy, 8, 16, 8)],
-                           E0.at[:, target_span(dx, 6, 16, hx), target_span(dy, 8, 16, 8)],
-                           s_e0.at[n], r_e0.at[n], (dx, dy, dz)))
-        else:
+        if dz != 0:
             side = 0 if dz > 0 else 1
             e0.append(send(M0.at[source_span(dx, 0, 8, 2), source_span(dy, 0, 16, 8)],
                            ZR0.at[side, target_span(dx, 2, 8, 2), target_span(dy, 8, 16, 8)],
                            s_e0.at[n], r_e0.at[n], (dx, dy, dz)))
+
+    PD[...] = jnp.zeros_like(PD)
+    B2[...] = jnp.zeros_like(B2)
+    V1[...] = jnp.zeros_like(V1)
+    PB1[...] = jnp.zeros_like(PB1)
 
     for k, a in ((0, 1), (1, 3)):
         sums = jnp.stack([E0[a, 6 + 2 * x, pl.ds(8, 16), :] + E0[a, 7 + 2 * x, pl.ds(8, 16), :] for x in range(8)])
@@ -195,10 +210,9 @@
             own = C1[k, 8 + x, pl.ds(8, 8), :]
             C1[k, 8 + x, pl.ds(8, 8), :] = jnp.where(
                 lane8 < 32, RZ1[0, k, x], jnp.where(lane8 < 96, own, RZ1[1, k, x]))
-    c1 = [send(C1.at[:, source_span(dx, 8, 8, 8), source_span(dy, 8, 8, 8)],
-               C1.at[:, target_span(dx, 8, 8, 8), target_span(dy, 8, 8, 8)],
+    c1 = [send(C1.at[:, source_span(dx, 8, 8, 4), source_span(dy, 8, 8, 8)],
+               C1.at[:, target_span(dx, 8, 8, 4), target_span(dy, 8, 8, 8)],
                s_c1.at[n], r_c1.at[n], (dx, dy, 0)) for n, (dx, dy, _) in enumerate(XY8)]
-
     def around(O, tiles, c, i, r0, q):
         out = []
         centre = [O[t, 1 - c, i + 1, pl.ds(r0, 24), :] for t in range(tiles)]
@@ -218,7 +232,7 @@
             out.append((centre[t], other, yp, ym, zp, zm))
         return out
 
-    def coefficients(PB, A, D, DG, tiles, r0, scale, shift_of, mask, x_of):
+    def coefficients(PB, A, D, DG, tiles, r0, scale, shift_of, mask, x_of, lo=0, hi=12):
         for c in range(2):
             def body(i, carry):
                 near = around(PB, tiles, c, i, r0, q24)
@@ -234,7 +248,7 @@
                     for k, w in enumerate(weights):
                         A[t, c, k, i] = w * inverse
                 return carry
-            lax.fori_loop(0, 12, body, 0)
+            loop(lo, hi, body, 0, 2)
 
     def relaxed(V, A, FD, tiles, c, i, r0):
         near = around(V, tiles, c, i, r0, q24)
@@ -247,12 +261,16 @@
         return out
 
     def half(V, A, FD, tiles, c, r0, lo, hi):
-        def body(i, carry):
-            new = relaxed(V, A, FD, tiles, c, i, r0)
-            for t in range(tiles):
-                V[t, c, i + 1, pl.ds(r0, 24), :] = new[t]
+        unroll = 4 if tiles == 1 else 2
+
+        def body(k, carry):
+            first = lo + k * unroll
+            news = [relaxed(V, A, FD, tiles, c, first + j, r0) for j in range(unroll)]
+            for j, new in enumerate(news):
+                for t in range(tiles):
+                    V[t, c, first + j + 1, pl.ds(r0, 24), :] = new[t]
             return carry
-        lax.fori_loop(lo, hi, body, 0)
+        lax.fori_loop(0, (hi - lo) // unroll, body, 0)
 
     def sweeps(V, A, FD, tiles, r0, lo=0, hi=12, first=0):
         for step in range(first, 4):
@@ -288,7 +306,7 @@
             dst[0, 1, p] = jnp.where(q32, even, odd) * m
         return carry
 
-    lax.fori_loop(0, 14, pack0, 0)
+    loop(0, 14, pack0, 0, 2)
     for p in (0, 13):
         for dst in (V0, PB0):
             for c in range(2):
@@ -310,7 +328,7 @@
             dst[0, 1, p - 1] = jnp.where(q24, even, odd)
         return carry
 
-    lax.fori_loop(1, 13, pack0_edge, 0)
+    loop(1, 13, pack0_edge, 0, 2)
     coefficients(PB0, A0, D0, DG0, 2, 4, 1.0, lambda t, c, i: DG0[t, c, i], mask0, x0)
 
     def scale_rhs0(i, carry):
@@ -319,14 +337,40 @@
                 FD0[t, c, i] = FD0[t, c, i] * D0[t, c, i]
         return carry
 
-    lax.fori_loop(0, 12, scale_rhs0, 0)
+    loop(0, 12, scale_rhs0, 0, 4)
+    wait(gc1)
+    gc2 = [send(GC.at[mine], GC.at[mine], s_gc2.at[n], r_gc2.at[n], o) for n, o in enumerate(ROW3)]
     sweeps(V0, A0, FD0, 2, 4)
 
     sums = []
     for i in range(2, 10):
         red, black = residual_pair(V0, A0, FD0, DG0, 2, i, 4)
         sums.append((red + black)[4:20])
-    S1[pl.ds(8, 8), pl.ds(8, 8)] = restrict_one(jnp.stack(sums))
+    own = restrict_one(jnp.stack(sums))
+    wait(c1)
+
+    def pack1(p, carry):
+        xs = x1(p)
+        m = mask1[0][8:32] * xs
+        even, odd = C1[1, 2 * p - 2], C1[1, 2 * p - 1]
+        PB1[0, 0, p, pl.ds(8, 24), :] = jnp.where(q24, odd, even) * m
+        PB1[0, 1, p, pl.ds(8, 24), :] = jnp.where(q24, even, odd) * m
+        even, odd = C1[0, 2 * p - 2], C1[0, 2 * p - 1]
+        DG1[0, 0, p - 1] = jnp.where(q24, odd, even)
+        DG1[0, 1, p - 1] = jnp.where(q24, even, odd)
+        return carry
+
+    def coefficients1(lo, hi):
+        loop(lo + 1, hi + 1, pack1, 0, 4)
+        coefficients(PB1, A1, D1, DG1, 1, 8, 0.25, lambda t, c, i: DG1[t, c, i], mask1, x1, lo, hi)
+
+    coefficients1(2, 10)
+    q8 = (iota((8, 128), 0) + iota((8, 128), 1)) % 2 == 1
+    for i in range(4, 8):
+        even, odd = own[2 * i - 8], own[2 * i - 7]
+        red = jnp.where(q8, odd, even) * D1[0, 0, i, pl.ds(8, 8), :]
+        black = jnp.where(q8, even, odd) * D1[0, 1, i, pl.ds(8, 8), :]
+        S1[2 * i, pl.ds(8, 8)], S1[2 * i + 1, pl.ds(8, 8)] = unpack(red, black, q8)
     slot = iota((8, 128), 1) // 16
     for g in range(2):
         total = jnp.zeros((8, 128), F32)
@@ -346,8 +390,6 @@
                            ZR1.at[side, target_span(dx, 1, 2, 1), target_span(dy, 8, 8, 8)],
                            s_e2.at[n], r_e2.at[n], (dx, dy, dz)))
 
-    wait(gc1)
-    gc2 = [send(GC.at[mine], GC.at[mine], s_gc2.at[n], r_gc2.at[n], o) for n, o in enumerate(PLANE31)]
     for i in range(2, 10):
         red, black = V0[0, 0, i + 1, pl.ds(8, 16), :], V0[0, 1, i + 1, pl.ds(8, 16), :]
         EU[0, 2 * i + 2, pl.ds(8, 16)], EU[0, 2 * i + 3, pl.ds(8, 16)] = unpack(red, black, q16)
@@ -358,22 +400,12 @@
         MU[g] = total
     uz = [send(MU, ZU.at[n], s_uz.at[n], r_uz.at[n], (0, 0, 1 if n == 0 else -1)) for n in range(2)]
 
-    wait(c1)
-
-    def pack1(p, carry):
-        xs = x1(p)
-        m = mask1[0][8:32] * xs
-        even, odd = C1[1, 2 * p - 2], C1[1, 2 * p - 1]
-        PB1[0, 0, p, pl.ds(8, 24), :] = jnp.where(q24, odd, even) * m
-        PB1[0, 1, p, pl.ds(8, 24), :] = jnp.where(q24, even, odd) * m
-        even, odd = C1[0, 2 * p - 2], C1[0, 2 * p - 1]
-        DG1[0, 0, p - 1] = jnp.where(q24, odd, even)
-        DG1[0, 1, p - 1] = jnp.where(q24, even, odd)
-        return carry
-
-    lax.fori_loop(1, 13, pack1, 0)
-    coefficients(PB1, A1, D1, DG1, 1, 8, 0.25, lambda t, c, i: DG1[t, c, i], mask1, x1)
-
+    wait(gc2)
+    row_of = GC.at[pl.ds(gy * 4, 4)]
+    gc3 = [send(row_of, row_of, s_gc3.at[n], r_gc3.at[n], o) for n, o in enumerate(CHIPS3)]
+    c1b = [send(C1.at[:, source_span(-dx, 8, 8, 4), source_span(dy, 8, 8, 8)],
+                C1.at[:, pl.ds(0 if dx > 0 else 20, 4), target_span(dy, 8, 8, 8)],
+                s_c1b.at[n], r_c1b.at[n], (dx, dy, 0)) for n, (dx, dy, _) in enumerate(X6)]
     wait(e2)
     slot24 = lane24 // 16
     for x in range(4, 20):
@@ -386,10 +418,11 @@
     def rhs1(source, lo, hi):
         def body(i, carry):
             even, odd = source[2 * i], source[2 * i + 1]
-            FD1[0, 0, i] = jnp.where(q24, odd, even) * D1[0, 0, i]
-            FD1[0, 1, i] = jnp.where(q24, even, odd) * D1[0, 1, i]
+            m = mask1[0][8:32] * x1(i + 1)
+            FD1[0, 0, i] = jnp.where(q24, odd, even) * m
+            FD1[0, 1, i] = jnp.where(q24, even, odd) * m
             return carry
-        lax.fori_loop(lo, hi, body, 0)
+        loop(lo, hi, body, 0, 4)
 
     rhs1(S1, 2, 10)
     for i in range(2, 10):
@@ -402,22 +435,24 @@
     GS[mine, gx] = restrict_two(jnp.stack(sums))
     gs1 = [send(GS.at[mine, gx], GS.at[mine, gx], s_gs1.at[n], r_gs1.at[n], o) for n, o in enumerate(RING7)]
 
-    q8 = (iota((8, 128), 0) + iota((8, 128), 1)) % 2 == 1
+    wait(gc3)
+    gc4 = []
+    for n in range(4):
+        rows = GC.at[pl.ds((core + 2 * n) * 4, 4)]
+        gc4.append(send(rows, rows, s_gc4.at[n], r_gc4.at[n]))
     for i in range(4, 8):
         red, black = V1[0, 0, i + 1, pl.ds(16, 8), :], V1[0, 1, i + 1, pl.ds(16, 8), :]
         PS[0, 2 * i, pl.ds(8, 8)], PS[0, 2 * i + 1, pl.ds(8, 8)] = unpack(red, black, q8)
-    ps = [send(PS.at[:, source_span(dx, 8, 8, 8), source_span(dy, 8, 8, 8)],
-               PS.at[:, target_span(dx, 8, 8, 8), target_span(dy, 8, 8, 8)],
-               s_ps.at[n], r_ps.at[n], (dx, dy, 0)) for n, (dx, dy, _) in enumerate(XY8)]
     wait(uz)
     for x in range(16):
         merged = jnp.where(lane16 % 16 < 8, ZU[0, x // 8], ZU[1, x // 8])
         EU[1, 6 + x, pl.ds(8, 16)] = roll(merged, -(16 * (x % 8) + 8))
     wait(gs1)
-    gs2 = [send(GS.at[mine], GS.at[mine], s_gs2.at[n], r_gs2.at[n], o) for n, o in enumerate(PLANE31)]
-    eu = [send(EU.at[:, source_span(dx, 6, 16, 5), source_span(dy, 8, 16, 8)],
-               EU.at[:, target_span(dx, 6, 16, 5), target_span(dy, 8, 16, 8)],
-               s_u.at[n], r_u.at[n], (dx, dy, 0)) for n, (dx, dy, _) in enumerate(XY8)]
+    gs2 = [send(GS.at[mine], GS.at[mine], s_gs2.at[n], r_gs2.at[n], o) for n, o in enumerate(SAME15)]
+    gs3 = [send(GS.at[mine], GS.at[mine], s_gs3.at[15], r_gs3.at[15])]
+    ps = [send(PS.at[:, source_span(dx, 8, 8, 8), source_span(dy, 8, 8, 8)],
+               PS.at[:, target_span(dx, 8, 8, 8), target_span(dy, 8, 8, 8)],
+               s_ps.at[n], r_ps.at[n], (dx, dy, 0)) for n, (dx, dy, _) in enumerate(XY8)]
 
     lane_group = lane8 // 32
 
@@ -432,7 +467,7 @@
                         total = jnp.where(lane_group == k, roll(blocks[k], 32 * (k - x)), total)
                     store(4 * g + x, 8 * pair, total)
             return carry
-        lax.fori_loop(0, 8, body, 0)
+        loop(0, 8, body, 0, 2)
 
     def store_s2(x, y, v):
         S2[x, pl.ds(y, 8), :] = v
@@ -444,7 +479,7 @@
         PD[x + 4, pl.ds(y + 8, 8), :] = v
         RM[x, pl.ds(y, 8), :] = v
 
-    wait(gc2)
+    wait(gc4)
     spread(lambda j, g: GC[j, g, 0], store_s2)
     spread(lambda j, g: GC[j, g, 1], store_b2)
 
@@ -471,34 +506,19 @@
         DG2[x] = total
         return carry
 
-    lax.fori_loop(0, 32, weights2, 0)
-
-    wait(ps)
-
-    def pack1_post(p, carry):
-        m = mask1[0][8:32] * x1(p)
-        even, odd = PS[0, 2 * p - 2], PS[0, 2 * p - 1]
-        V1[0, 0, p, pl.ds(8, 24), :] = jnp.where(q24, odd, even) * m
-        V1[0, 1, p, pl.ds(8, 24), :] = jnp.where(q24, even, odd) * m
-        return carry
-
-    lax.fori_loop(1, 13, pack1_post, 0)
-    rhs1(PS.at[1], 0, 12)
-
-    wait(eu)
-
-    def pack0_post(p, carry):
-        xs = x0(p)
-        for t in range(2):
-            m = mask0[t] * xs
-            even, odd = EU[t, 2 * p], EU[t, 2 * p + 1]
-            V0[t, 0, p] = jnp.where(q32, odd, even) * m
-            V0[t, 1, p] = jnp.where(q32, even, odd) * m
-        return carry
-
-    lax.fori_loop(0, 14, pack0_post, 0)
-
-    wait(gs2)
+    loop(0, 32, weights2, 0, 4)
+
+    wait(c1b)
+    coefficients1(0, 12)
+
+    for n, (_, j, k) in enumerate(SAME15):
+        gs2[n].wait()
+        came = GS.at[lax.rem(gy + 8 - j, 8) * 4 + lax.rem(gz + 4 - k, 4)]
+        gs3.append(send(came, came, s_gs3.at[n], r_gs3.at[n]))
+    wait(gs3)
+    eu = [send(EU.at[:, source_span(dx, 6, 16, 5), source_span(dy, 8, 16, 8)],
+               EU.at[:, target_span(dx, 6, 16, 5), target_span(dy, 8, 16, 8)],
+               s_u.at[n], r_u.at[n], (dx, dy, 0)) for n, (dx, dy, _) in enumerate(XY8)]
     spread(lambda j, g: GS[j, g], store_source)
     XL[...] = jnp.zeros_like(XL)
 
@@ -509,7 +529,7 @@
         return total + RM[x] * RM[x]
 
     acc = jnp.zeros((32, 128), F32)
-    rr = whole(lax.fori_loop(0, 32, square, acc))
+    rr = whole(loop(0, 32, square, acc, 8))
     for step in range(CG_ITERS):
         def image(x, total):
             p, near = shifts(PD, x)
@@ -519,28 +539,53 @@
             AP[x] = value
             return total + p * value
 
-        alpha = rr / whole(lax.fori_loop(0, 32, image, acc))
+        alpha = rr / whole(loop(0, 32, image, acc, 8))
 
         def gain(x, carry):
             XL[x] = XL[x] + alpha * PD[4 * gx + x, pl.ds(4 * gy + 4, 16), :]
             return carry
 
-        lax.fori_loop(0, 12, gain, 0)
+        loop(0, 12, gain, 0, 12)
         if step < CG_ITERS - 1:
             def update(x, total):
                 value = RM[x] - alpha * AP[x]
                 RM[x] = value
                 return total + value * value
 
-            new = whole(lax.fori_loop(0, 32, update, acc))
+            new = whole(loop(0, 32, update, acc, 8))
             ratio = new / rr
 
             def turn(x, carry):
                 PD[x + 4, pl.ds(8, 32), :] = RM[x] + ratio * PD[x + 4, pl.ds(8, 32), :]
                 return carry
 
-            lax.fori_loop(0, 32, turn, 0)
+            loop(0, 32, turn, 0, 8)
             rr = new
+
+    wait(ps)
+
+    def pack1_post(p, carry):
+        m = mask1[0][8:32] * x1(p)
+        even, odd = PS[0, 2 * p - 2], PS[0, 2 * p - 1]
+        V1[0, 0, p, pl.ds(8, 24), :] = jnp.where(q24, odd, even) * m
+        V1[0, 1, p, pl.ds(8, 24), :] = jnp.where(q24, even, odd) * m
+        return carry
+
+    loop(1, 13, pack1_post, 0, 4)
+    rhs1(PS.at[1], 0, 12)
+
+    wait(eu)
+
+    def pack0_post(p, carry):
+        xs = x0(p)
+        for t in range(2):
+            m = mask0[t] * xs
+            even, odd = EU[t, 2 * p], EU[t, 2 * p + 1]
+            V0[t, 0, p] = jnp.where(q32, odd, even) * m
+            V0[t, 1, p] = jnp.where(q32, even, odd) * m
+        return carry
+
+    loop(0, 14, pack0_post, 0, 2)
 
     fine = pick(XL[...].reshape(192, 128), from_two).reshape(12, 16, 128)
     X16[:, pl.ds(0, 16, stride=2), :] = fine
@@ -551,7 +596,7 @@
             V1[0, c, i + 1, pl.ds(8, 24), :] = V1[0, c, i + 1, pl.ds(8, 24), :] + X16[i, 0:24]
         return carry
 
-    lax.fori_loop(0, 12, correct1, 0)
+    loop(0, 12, correct1, 0, 4)
     sweeps(V1, A1, FD1, 1, 8)
 
     planes = []
@@ -570,7 +615,7 @@
                 V0[t, c, p] = V0[t, c, p] + XB[p]
             return carry
 
-        lax.fori_loop(0, 14, correct0, 0)
+        loop(0, 14, correct0, 0, 2)
     sweeps(V0, A0, FD0, 2, 4)
 
     def finish(i, carry):
@@ -583,7 +628,7 @@
         x_out[2 * i - 3] = odd
         return carry
 
-    lax.fori_loop(2, 10, finish, 0)
+    loop(2, 10, finish, 0, 2)
 
 
 def vmem(*shape):
@@ -608,7 +653,8 @@
     vmem(32, 32, 128), vmem(40, 48, 128), vmem(6, 32, 32, 128), vmem(32, 32, 128),
     vmem(40, 48, 128), vmem(32, 32, 128), vmem(32, 32, 128), vmem(12, 16, 128),
     dma(4), dma(26), dma(26), dma(2), dma(2), dma(8), dma(8), dma(26), dma(26), dma(2), dma(2), dma(8), dma(8),
-    dma(8), dma(8), dma(7), dma(7), dma(31), dma(31), dma(7), dma(7), dma(31), dma(31),
+    dma(8), dma(8), dma(7), dma(7), dma(3), dma(3), dma(7), dma(7), dma(15), dma(15),
+    dma(3), dma(3), dma(4), dma(4), dma(16), dma(16), dma(6), dma(6),
 ]
 
 

time: 102 us -> 67.5 us (0.66)
  Pallas kernels: 98.8 us -> 64.5 us
    pallas_call x1, Pallas kernels: 98.8 us -> 64.5 us  [local(): pl.pallas_call(kernel, out_shape=(shape, shape), in_specs=[pl.BlockSpec(m...]
where the time goes in v2:
time: 67.5 us; the launch traced here: 67.4 us
  Pallas kernels  64.5 us (96%)
  local copies, waits for them, and re-layouts  2.26 us (3%)
    pallas_call x1, Pallas kernels, local(): pl.pallas_call(kernel, out_shape=(shape, shape), in_specs=[pl.BlockSpec(m...  64.5 us
    unnamed x4, local copies, waits for them, and re-layouts  2.26 us

profile of v2, /device:TPU:1, one launch (start us, length us, event | category | flops | bytes accessed | tf_op | source)
XLA Modules:
  0.0 67.4 jit_solution(781456520344352179)
XLA Ops:
  0.6 64.5 %shard_map.59 = (f32[16,16,128]{2,1,0:T(8,128)}, f32[16,16,128]{2,1,0:T(8,128)}) custom-call(f32[16,16,128]{2,1,0:T(8,128)} %f_in.1, f32[16,16,128]{2,1,0:T(8,128)} %u_in.1, f32[16,16,128]{2,1,0:T(8,128)} %s_in.1, f32[16,16,128]{2,1,0:T(8,128)} %b_in.1), custom_call_target="tpu_custom_call" | custom-call | tf_op jit(solution)/shard_map/pallas_call | solution.py:664
  65.1 0.0 copy-start
  65.1 1.6 %copy.8 = f32[16,16,128]{2,1,0:T(8,128)} copy(f32[16,16,128]{2,1,0:T(8,128)} %get-tuple-element.4) | data formatting | bytes 262144
  66.7 0.0 copy-done
  66.7 0.7 copy.9
Async XLA Ops:
  65.1 1.6 %copy-start = (f32[16,16,128]{2,1,0:T(8,128)S(1)}, f32[16,16,128]{2,1,0:T(8,128)}, u32[]{:S(2)}) copy-start(f32[16,16,128]{2,1,0:T(8,128)} %get-tuple-element.5) | copy-start | bytes 393220

commit v3 on v2

--- a/solution.py
+++ b/solution.py
@@ -14,8 +14,11 @@
 F32 = jnp.float32
 BF16 = jnp.bfloat16
 
-ALL26 = [o for o in itertools.product((-1, 0, 1), repeat=3) if o != (0, 0, 0)]
+ALL26 = sorted((o for o in itertools.product((-1, 0, 1), repeat=3) if o != (0, 0, 0)),
+               key=lambda o: -sum(map(abs, o)))
 XY8 = [o for o in ALL26 if o[2] == 0]
+XY4 = [o for o in XY8 if o[0] * o[1] == 0]
+CORNERS = [o for o in XY8 if o[0] * o[1] != 0]
 X6 = [o for o in XY8 if o[0] != 0]
 RING7 = [(k, 0, 0) for k in range(1, 8)]
 ROW3 = [(0, 0, k) for k in range(1, 4)]
@@ -71,12 +74,13 @@
     return value if shift == 0 else pltpu.roll(value, shift, 1)
 
 
-def kernel(f_in, u_in, s_in, b_in, x_out, r_out, E0, M0, ZR0, V0, PB0, A0, D0, DG0, FD0,
+def kernel(f_in, u_in, s_in, b_in, x_out, r_out, E0, M0, MX, RZ0, CP, CR, V0, PB0, A0, D0, DG0, FD0,
            C1, R1s, RZ1, S1, M1, ZR1, PS, V1, PB1, A1, D1, DG1, FD1,
            EU, MU, ZU, T16, T8, T4, X16, XB, GC, GS, S2, B2, A2, DG2, PD, RM, AP, XL,
            sem_in, s_e0, r_e0, s_c1z, r_c1z, s_c1, r_c1, s_e2, r_e2, s_uz, r_uz, s_u, r_u,
            s_ps, r_ps, s_gc1, r_gc1, s_gc2, r_gc2, s_gs1, r_gs1, s_gs2, r_gs2,
-           s_gc3, r_gc3, s_gc4, r_gc4, s_gs3, r_gs3, s_c1b, r_c1b):
+           s_gc3, r_gc3, s_gc4, r_gc4, s_gs3, r_gs3, s_c1b, r_c1b,
+           s_z0, r_z0, s_mx, r_mx):
     gx, gy, gz = (lax.axis_index(a) for a in AXES)
     me = (gx, gy, gz)
     core = lax.rem(gy, 2)
@@ -159,13 +163,22 @@
     for copy in local:
         copy.wait()
     pl.semaphore_wait(barrier, len(PARTNERS))
-    e0 = []
-    for n, (dx, dy, dz) in enumerate(ALL26):
-        if dz == 0:
-            hx = 4 if dx and dy else 5
-            e0.append(send(E0.at[:, source_span(dx, 6, 16, hx), source_span(dy, 8, 16, 8)],
-                           E0.at[:, target_span(dx, 6, 16, hx), target_span(dy, 8, 16, 8)],
-                           s_e0.at[n], r_e0.at[n], (dx, dy, dz)))
+    e0 = [send(E0.at[:, source_span(dx, 6, 16, 5), source_span(dy, 8, 16, 8)],
+               E0.at[:, target_span(dx, 6, 16, 5), target_span(dy, 8, 16, 8)],
+               s_e0.at[n], r_e0.at[n], (dx, dy, 0)) for n, (dx, dy, _) in enumerate(XY4)]
+
+    upper = iota((8, 128), 0) < 4
+    for n, (dx, dy, _) in enumerate(CORNERS):
+        x, y = (18 if dx > 0 else 6), (16 if dy > 0 else 8)
+        for a in range(4):
+            for k in range(2):
+                first, second = E0[a, x + 2 * k, pl.ds(y, 8), :], E0[a, x + 2 * k + 1, pl.ds(y, 8), :]
+                if dy > 0:
+                    first = pltpu.roll(first, 4, 0)
+                else:
+                    second = pltpu.roll(second, 4, 0)
+                CP[n, a, k] = jnp.where(upper, first, second)
+        e0.append(send(CP.at[n], CR.at[n], s_e0.at[4 + n], r_e0.at[4 + n], (dx, dy, 0)))
 
     lane16 = iota((16, 128), 1)
     group = lane16 // 16
@@ -180,12 +193,7 @@
         return carry
 
     loop(0, 8, pack_rows, 0, 4)
-    for n, (dx, dy, dz) in enumerate(ALL26):
-        if dz != 0:
-            side = 0 if dz > 0 else 1
-            e0.append(send(M0.at[source_span(dx, 0, 8, 2), source_span(dy, 0, 16, 8)],
-                           ZR0.at[side, target_span(dx, 2, 8, 2), target_span(dy, 8, 16, 8)],
-                           s_e0.at[n], r_e0.at[n], (dx, dy, dz)))
+    z0 = [send(M0, RZ0.at[n], s_z0.at[n], r_z0.at[n], (0, 0, 1 if n == 0 else -1)) for n in range(2)]
 
     PD[...] = jnp.zeros_like(PD)
     B2[...] = jnp.zeros_like(B2)
@@ -203,6 +211,12 @@
         sums = jnp.stack([C1[k, 8 + 2 * x, pl.ds(8, 8), :] + C1[k, 9 + 2 * x, pl.ds(8, 8), :] for x in range(4)])
         GC[mine, gx, k] = restrict_two(sums)
     gc1 = [send(GC.at[mine, gx], GC.at[mine, gx], s_gc1.at[n], r_gc1.at[n], o) for n, o in enumerate(RING7)]
+    wait(z0)
+    for k in range(8):
+        MX[2 + k, pl.ds(8, 16)] = jnp.where(lane16 % 16 < 8, RZ0[0, k], RZ0[1, k])
+    mx = [send(MX.at[source_span(dx, 2, 8, 2), source_span(dy, 8, 16, 8)],
+               MX.at[target_span(dx, 2, 8, 2), target_span(dy, 8, 16, 8)],
+               s_mx.at[n], r_mx.at[n], (dx, dy, 0)) for n, (dx, dy, _) in enumerate(XY8)]
     wait(c1z)
     lane8 = iota((8, 128), 1)
     for k in range(2):
@@ -261,7 +275,7 @@
         return out
 
     def half(V, A, FD, tiles, c, r0, lo, hi):
-        unroll = 4 if tiles == 1 else 2
+        unroll = 4 if tiles == 1 else 4
 
         def body(k, carry):
             first = lo + k * unroll
@@ -287,11 +301,17 @@
         return jnp.where(q, black, red), jnp.where(q, red, black)
 
     wait(e0)
+    for n, (dx, dy, _) in enumerate(CORNERS):
+        x, y = (2 if dx > 0 else 22), (4 if dy > 0 else 24)
+        for a in range(4):
+            for k in range(4):
+                E0[a, x + k, pl.ds(y, 4), :] = CR[n, a, k // 2, pl.ds(4 * (k % 2), 4), :]
+    wait(mx)
 
     lane32 = iota((32, 128), 1)
 
     def edge_of(a, p):
-        merged = jnp.where(lane32 % 16 < 8, ZR0[0, p - 1], ZR0[1, p - 1])
+        merged = MX[p - 1]
         return roll(merged, -(16 * a + 8)), roll(merged, -(16 * a + 72))
 
     x0 = lambda p: x_scalar(p, 3, 11)
@@ -539,7 +559,7 @@
             AP[x] = value
             return total + p * value
 
-        alpha = rr / whole(loop(0, 32, image, acc, 8))
+        alpha = rr / whole(loop(0, 32, image, acc, 16))
 
         def gain(x, carry):
             XL[x] = XL[x] + alpha * PD[4 * gx + x, pl.ds(4 * gy + 4, 16), :]
@@ -552,14 +572,14 @@
                 RM[x] = value
                 return total + value * value
 
-            new = whole(loop(0, 32, update, acc, 8))
+            new = whole(loop(0, 32, update, acc, 16))
             ratio = new / rr
 
             def turn(x, carry):
                 PD[x + 4, pl.ds(8, 32), :] = RM[x] + ratio * PD[x + 4, pl.ds(8, 32), :]
                 return carry
 
-            loop(0, 32, turn, 0, 8)
+            loop(0, 32, turn, 0, 16)
             rr = new
 
     wait(ps)
@@ -640,7 +660,8 @@
 
 
 SCRATCH = [
-    vmem(4, 28, 32, 128), vmem(8, 16, 128), vmem(2, 12, 32, 128),
+    vmem(4, 28, 32, 128), vmem(8, 16, 128), vmem(12, 32, 128), vmem(2, 8, 16, 128),
+    vmem(4, 4, 2, 8, 128), vmem(4, 4, 2, 8, 128),
     vmem(2, 2, 14, 32, 128), vmem(2, 2, 14, 32, 128), vmem(2, 2, 6, 12, 24, 128),
     vmem(2, 2, 12, 24, 128), vmem(2, 2, 12, 24, 128), vmem(2, 2, 12, 24, 128),
     vmem(2, 24, 24, 128), vmem(2, 8, 8, 128), vmem(2, 2, 8, 8, 128),
@@ -652,9 +673,10 @@
     vmem(32, 8, 2, 4, 128), vmem(32, 8, 4, 128),
     vmem(32, 32, 128), vmem(40, 48, 128), vmem(6, 32, 32, 128), vmem(32, 32, 128),
     vmem(40, 48, 128), vmem(32, 32, 128), vmem(32, 32, 128), vmem(12, 16, 128),
-    dma(4), dma(26), dma(26), dma(2), dma(2), dma(8), dma(8), dma(26), dma(26), dma(2), dma(2), dma(8), dma(8),
+    dma(4), dma(8), dma(8), dma(2), dma(2), dma(8), dma(8), dma(26), dma(26), dma(2), dma(2), dma(8), dma(8),
     dma(8), dma(8), dma(7), dma(7), dma(3), dma(3), dma(7), dma(7), dma(15), dma(15),
     dma(3), dma(3), dma(4), dma(4), dma(16), dma(16), dma(6), dma(6),
+    dma(2), dma(2), dma(8), dma(8),
 ]
 
 

time: 67.5 us -> 61.9 us (0.917)
  Pallas kernels: 64.5 us -> 58.8 us
    pallas_call x1, Pallas kernels: 64.5 us -> 58.8 us  [local(): pl.pallas_call(kernel, out_shape=(shape, shape), in_specs=[pl.BlockSpec(m...]
where the time goes in v3:
time: 61.9 us; the launch traced here: 61.7 us
  Pallas kernels  58.8 us (95%)
  local copies, waits for them, and re-layouts  2.26 us (4%)
  between operations  0.65 us (1%)
    pallas_call x1, Pallas kernels, local(): pl.pallas_call(kernel, out_shape=(shape, shape), in_specs=[pl.BlockSpec(m...  58.8 us
    unnamed x4, local copies, waits for them, and re-layouts  2.26 us

profile of v3, /device:TPU:1, one launch (start us, length us, event | category | flops | bytes accessed | tf_op | source)
XLA Modules:
  0.0 61.7 jit_solution(7404748015581489375)
XLA Ops:
  0.6 58.8 %shard_map.59 = (f32[16,16,128]{2,1,0:T(8,128)}, f32[16,16,128]{2,1,0:T(8,128)}) custom-call(f32[16,16,128]{2,1,0:T(8,128)} %f_in.1, f32[16,16,128]{2,1,0:T(8,128)} %u_in.1, f32[16,16,128]{2,1,0:T(8,128)} %s_in.1, f32[16,16,128]{2,1,0:T(8,128)} %b_in.1), custom_call_target="tpu_custom_call" | custom-call | tf_op jit(solution)/shard_map/pallas_call | solution.py:686
  59.5 0.0 copy-start
  59.5 1.6 %copy.8 = f32[16,16,128]{2,1,0:T(8,128)} copy(f32[16,16,128]{2,1,0:T(8,128)} %get-tuple-element.4) | data formatting | bytes 262144
  61.1 0.0 copy-done
  61.1 0.7 %copy.9 = f32[16,16,128]{2,1,0:T(8,128)} copy(f32[16,16,128]{2,1,0:T(8,128)S(1)} %copy-done) | data formatting | bytes 262144
Async XLA Ops:
  59.5 1.6 %copy-start = (f32[16,16,128]{2,1,0:T(8,128)S(1)}, f32[16,16,128]{2,1,0:T(8,128)}, u32[]{:S(2)}) copy-start(f32[16,16,128]{2,1,0:T(8,128)} %get-tuple-element.5) | copy-start | bytes 393220

commit v4 on v3

--- a/solution.py
+++ b/solution.py
@@ -162,11 +162,6 @@
 
     for copy in local:
         copy.wait()
-    pl.semaphore_wait(barrier, len(PARTNERS))
-    e0 = [send(E0.at[:, source_span(dx, 6, 16, 5), source_span(dy, 8, 16, 8)],
-               E0.at[:, target_span(dx, 6, 16, 5), target_span(dy, 8, 16, 8)],
-               s_e0.at[n], r_e0.at[n], (dx, dy, 0)) for n, (dx, dy, _) in enumerate(XY4)]
-
     upper = iota((8, 128), 0) < 4
     for n, (dx, dy, _) in enumerate(CORNERS):
         x, y = (18 if dx > 0 else 6), (16 if dy > 0 else 8)
@@ -178,7 +173,6 @@
                 else:
                     second = pltpu.roll(second, 4, 0)
                 CP[n, a, k] = jnp.where(upper, first, second)
-        e0.append(send(CP.at[n], CR.at[n], s_e0.at[4 + n], r_e0.at[4 + n], (dx, dy, 0)))
 
     lane16 = iota((16, 128), 1)
     group = lane16 // 16
@@ -193,12 +187,13 @@
         return carry
 
     loop(0, 8, pack_rows, 0, 4)
+    pl.semaphore_wait(barrier, len(PARTNERS))
     z0 = [send(M0, RZ0.at[n], s_z0.at[n], r_z0.at[n], (0, 0, 1 if n == 0 else -1)) for n in range(2)]
-
-    PD[...] = jnp.zeros_like(PD)
-    B2[...] = jnp.zeros_like(B2)
-    V1[...] = jnp.zeros_like(V1)
-    PB1[...] = jnp.zeros_like(PB1)
+    e0 = [send(E0.at[:, source_span(dx, 6, 16, 5), source_span(dy, 8, 16, 8)],
+               E0.at[:, target_span(dx, 6, 16, 5), target_span(dy, 8, 16, 8)],
+               s_e0.at[n], r_e0.at[n], (dx, dy, 0)) for n, (dx, dy, _) in enumerate(XY4)]
+    for n, (dx, dy, _) in enumerate(CORNERS):
+        e0.append(send(CP.at[n], CR.at[n], s_e0.at[4 + n], r_e0.at[4 + n], (dx, dy, 0)))
 
     for k, a in ((0, 1), (1, 3)):
         sums = jnp.stack([E0[a, 6 + 2 * x, pl.ds(8, 16), :] + E0[a, 7 + 2 * x, pl.ds(8, 16), :] for x in range(8)])
@@ -224,9 +219,6 @@
             own = C1[k, 8 + x, pl.ds(8, 8), :]
             C1[k, 8 + x, pl.ds(8, 8), :] = jnp.where(
                 lane8 < 32, RZ1[0, k, x], jnp.where(lane8 < 96, own, RZ1[1, k, x]))
-    c1 = [send(C1.at[:, source_span(dx, 8, 8, 4), source_span(dy, 8, 8, 8)],
-               C1.at[:, target_span(dx, 8, 8, 4), target_span(dy, 8, 8, 8)],
-               s_c1.at[n], r_c1.at[n], (dx, dy, 0)) for n, (dx, dy, _) in enumerate(XY8)]
     def around(O, tiles, c, i, r0, q):
         out = []
         centre = [O[t, 1 - c, i + 1, pl.ds(r0, 24), :] for t in range(tiles)]
@@ -262,7 +254,7 @@
                     for k, w in enumerate(weights):
                         A[t, c, k, i] = w * inverse
                 return carry
-            loop(lo, hi, body, 0, 2)
+            loop(lo, hi, body, 0, 4)
 
     def relaxed(V, A, FD, tiles, c, i, r0):
         near = around(V, tiles, c, i, r0, q24)
@@ -274,8 +266,7 @@
             out.append(total)
         return out
 
-    def half(V, A, FD, tiles, c, r0, lo, hi):
-        unroll = 4 if tiles == 1 else 4
+    def half(V, A, FD, tiles, c, r0, lo, hi, unroll):
 
         def body(k, carry):
             first = lo + k * unroll
@@ -286,9 +277,9 @@
             return carry
         lax.fori_loop(0, (hi - lo) // unroll, body, 0)
 
-    def sweeps(V, A, FD, tiles, r0, lo=0, hi=12, first=0):
+    def sweeps(V, A, FD, tiles, r0, spans, first=0):
         for step in range(first, 4):
-            half(V, A, FD, tiles, step % 2, r0, lo, hi)
+            half(V, A, FD, tiles, step % 2, r0, *spans[step // 2])
 
     def residual_pair(V, A, FD, DG, tiles, i, r0):
         out = []
@@ -300,6 +291,10 @@
     def unpack(red, black, q):
         return jnp.where(q, black, red), jnp.where(q, red, black)
 
+    PD[...] = jnp.zeros_like(PD)
+    B2[...] = jnp.zeros_like(B2)
+    V1[...] = jnp.zeros_like(V1)
+    PB1[...] = jnp.zeros_like(PB1)
     wait(e0)
     for n, (dx, dy, _) in enumerate(CORNERS):
         x, y = (2 if dx > 0 else 22), (4 if dy > 0 else 24)
@@ -307,6 +302,9 @@
             for k in range(4):
                 E0[a, x + k, pl.ds(y, 4), :] = CR[n, a, k // 2, pl.ds(4 * (k % 2), 4), :]
     wait(mx)
+    c1 = [send(C1.at[:, source_span(dx, 8, 8, 4), source_span(dy, 8, 8, 8)],
+               C1.at[:, target_span(dx, 8, 8, 4), target_span(dy, 8, 8, 8)],
+               s_c1.at[n], r_c1.at[n], (dx, dy, 0)) for n, (dx, dy, _) in enumerate(XY8)]
 
     lane32 = iota((32, 128), 1)
 
@@ -326,7 +324,7 @@
             dst[0, 1, p] = jnp.where(q32, even, odd) * m
         return carry
 
-    loop(0, 14, pack0, 0, 2)
+    loop(0, 14, pack0, 0, 7)
     for p in (0, 13):
         for dst in (V0, PB0):
             for c in range(2):
@@ -348,7 +346,7 @@
             dst[0, 1, p - 1] = jnp.where(q24, even, odd)
         return carry
 
-    loop(1, 13, pack0_edge, 0, 2)
+    loop(1, 13, pack0_edge, 0, 6)
     coefficients(PB0, A0, D0, DG0, 2, 4, 1.0, lambda t, c, i: DG0[t, c, i], mask0, x0)
 
     def scale_rhs0(i, carry):
@@ -360,7 +358,7 @@
     loop(0, 12, scale_rhs0, 0, 4)
     wait(gc1)
     gc2 = [send(GC.at[mine], GC.at[mine], s_gc2.at[n], r_gc2.at[n], o) for n, o in enumerate(ROW3)]
-    sweeps(V0, A0, FD0, 2, 4)
+    sweeps(V0, A0, FD0, 2, 4, ((0, 12, 4), (1, 11, 5)))
 
     sums = []
     for i in range(2, 10):
@@ -447,7 +445,7 @@
     rhs1(S1, 2, 10)
     for i in range(2, 10):
         V1[0, 0, i + 1, pl.ds(8, 24), :] = FD1[0, 0, i]
-    sweeps(V1, A1, FD1, 1, 8, 2, 10, first=1)
+    sweeps(V1, A1, FD1, 1, 8, ((2, 10, 4), (3, 9, 6)), first=1)
     sums = []
     for i in range(4, 8):
         red, black = residual_pair(V1, A1, FD1, DG1, 1, i, 8)
@@ -487,7 +485,7 @@
                         total = jnp.where(lane_group == k, roll(blocks[k], 32 * (k - x)), total)
                     store(4 * g + x, 8 * pair, total)
             return carry
-        loop(0, 8, body, 0, 2)
+        loop(0, 8, body, 0, 4)
 
     def store_s2(x, y, v):
         S2[x, pl.ds(y, 8), :] = v
@@ -526,7 +524,7 @@
         DG2[x] = total
         return carry
 
-    loop(0, 32, weights2, 0, 4)
+    loop(0, 32, weights2, 0, 8)
 
     wait(c1b)
     coefficients1(0, 12)
@@ -549,17 +547,39 @@
         return total + RM[x] * RM[x]
 
     acc = jnp.zeros((32, 128), F32)
+    RM[32] = acc
     rr = whole(loop(0, 32, square, acc, 8))
     for step in range(CG_ITERS):
-        def image(x, total):
-            p, near = shifts(PD, x)
-            value = DG2[x] * p
-            for k, v in enumerate(near):
-                value = value - A2[k, x] * v
-            AP[x] = value
-            return total + p * value
-
-        alpha = rr / whole(loop(0, 32, image, acc, 16))
+        def plane(x):
+            value = PD[x + 4, pl.ds(8, 32), :]
+            if step:
+                value = RM[x] + ratio * value
+                PD[x + 4, pl.ds(8, 32), :] = value
+            return value
+
+        if step:
+            plane(0)
+
+        def image(g, total):
+            start = 16 * g
+            before = PD[start + 3, pl.ds(8, 32), :]
+            weight = A2[1, start]
+            p = PD[start + 4, pl.ds(8, 32), :]
+            for j in range(16):
+                x = start + j
+                after = plane(x + 1)
+                value = DG2[x] * p - weight * before
+                weight = A2[0, x]
+                value = value - weight * after
+                value = value - A2[2, x] * PD[x + 4, pl.ds(9, 32), :]
+                value = value - A2[3, x] * PD[x + 4, pl.ds(7, 32), :]
+                value = value - A2[4, x] * roll(p, -1) - A2[5, x] * roll(p, 1)
+                AP[x] = value
+                total = total + p * value
+                before, p = p, after
+            return total
+
+        alpha = rr / whole(lax.fori_loop(0, 32 // 16, image, acc))
 
         def gain(x, carry):
             XL[x] = XL[x] + alpha * PD[4 * gx + x, pl.ds(4 * gy + 4, 16), :]
@@ -575,11 +595,6 @@
             new = whole(loop(0, 32, update, acc, 16))
             ratio = new / rr
 
-            def turn(x, carry):
-                PD[x + 4, pl.ds(8, 32), :] = RM[x] + ratio * PD[x + 4, pl.ds(8, 32), :]
-                return carry
-
-            loop(0, 32, turn, 0, 16)
             rr = new
 
     wait(ps)
@@ -616,8 +631,8 @@
             V1[0, c, i + 1, pl.ds(8, 24), :] = V1[0, c, i + 1, pl.ds(8, 24), :] + X16[i, 0:24]
         return carry
 
-    loop(0, 12, correct1, 0, 4)
-    sweeps(V1, A1, FD1, 1, 8)
+    loop(0, 12, correct1, 0, 12)
+    sweeps(V1, A1, FD1, 1, 8, ((1, 11, 5), (2, 10, 4)))
 
     planes = []
     for p in range(14):
@@ -635,8 +650,8 @@
                 V0[t, c, p] = V0[t, c, p] + XB[p]
             return carry
 
-        loop(0, 14, correct0, 0, 2)
-    sweeps(V0, A0, FD0, 2, 4)
+        loop(0, 14, correct0, 0, 7)
+    sweeps(V0, A0, FD0, 2, 4, ((0, 12, 4), (1, 11, 5)))
 
     def finish(i, carry):
         red, black = residual_pair(V0, A0, FD0, DG0, 2, i, 4)
@@ -648,7 +663,7 @@
         x_out[2 * i - 3] = odd
         return carry
 
-    loop(2, 10, finish, 0, 2)
+    loop(2, 10, finish, 0, 4)
 
 
 def vmem(*shape):
@@ -672,7 +687,7 @@
     vmem(8, 16, 128), vmem(4, 8, 128), vmem(4, 8, 128), vmem(12, 32, 128), vmem(14, 32, 128),
     vmem(32, 8, 2, 4, 128), vmem(32, 8, 4, 128),
     vmem(32, 32, 128), vmem(40, 48, 128), vmem(6, 32, 32, 128), vmem(32, 32, 128),
-    vmem(40, 48, 128), vmem(32, 32, 128), vmem(32, 32, 128), vmem(12, 16, 128),
+    vmem(40, 48, 128), vmem(33, 32, 128), vmem(32, 32, 128), vmem(12, 16, 128),
     dma(4), dma(8), dma(8), dma(2), dma(2), dma(8), dma(8), dma(26), dma(26), dma(2), dma(2), dma(8), dma(8),
     dma(8), dma(8), dma(7), dma(7), dma(3), dma(3), dma(7), dma(7), dma(15), dma(15),
     dma(3), dma(3), dma(4), dma(4), dma(16), dma(16), dma(6), dma(6),

time: 61.9 us -> 59.4 us (0.960)
  Pallas kernels: 58.8 us -> 56.4 us
    pallas_call x1, Pallas kernels: 58.8 us -> 56.4 us  [local(): pl.pallas_call(kernel, out_shape=(shape, shape), in_specs=[pl.BlockSpec(m...]
where the time goes in v4:
time: 59.4 us; the launch traced here: 59.3 us
  Pallas kernels  56.4 us (95%)
  local copies, waits for them, and re-layouts  2.26 us (4%)
  between operations  0.65 us (1%)
    pallas_call x1, Pallas kernels, local(): pl.pallas_call(kernel, out_shape=(shape, shape), in_specs=[pl.BlockSpec(m...  56.4 us
    unnamed x4, local copies, waits for them, and re-layouts  2.26 us

profile of v4, /device:TPU:1, one launch (start us, length us, event | category | flops | bytes accessed | tf_op | source)
XLA Modules:
  0.0 59.3 jit_solution(5325299958771364180)
XLA Ops:
  0.6 56.4 %shard_map.59 = (f32[16,16,128]{2,1,0:T(8,128)}, f32[16,16,128]{2,1,0:T(8,128)}) custom-call(f32[16,16,128]{2,1,0:T(8,128)} %f_in.1, f32[16,16,128]{2,1,0:T(8,128)} %u_in.1, f32[16,16,128]{2,1,0:T(8,128)} %s_in.1, f32[16,16,128]{2,1,0:T(8,128)} %b_in.1), custom_call_target="tpu_custom_call" | custom-call | tf_op jit(solution)/shard_map/pallas_call | solution.py:701
  57.0 0.0 copy-start
  57.0 1.6 %copy.8 = f32[16,16,128]{2,1,0:T(8,128)} copy(f32[16,16,128]{2,1,0:T(8,128)} %get-tuple-element.4) | data formatting | bytes 262144
  58.6 0.0 copy-done
  58.6 0.7 %copy.9 = f32[16,16,128]{2,1,0:T(8,128)} copy(f32[16,16,128]{2,1,0:T(8,128)S(1)} %copy-done) | data formatting | bytes 262144
Async XLA Ops:
  57.0 1.6 %copy-start = (f32[16,16,128]{2,1,0:T(8,128)S(1)}, f32[16,16,128]{2,1,0:T(8,128)}, u32[]{:S(2)}) copy-start(f32[16,16,128]{2,1,0:T(8,128)} %get-tuple-element.5) | copy-start | bytes 393220

commit v5 on v4

--- a/solution.py
+++ b/solution.py
@@ -19,7 +19,6 @@
 XY8 = [o for o in ALL26 if o[2] == 0]
 XY4 = [o for o in XY8 if o[0] * o[1] == 0]
 CORNERS = [o for o in XY8 if o[0] * o[1] != 0]
-X6 = [o for o in XY8 if o[0] != 0]
 RING7 = [(k, 0, 0) for k in range(1, 8)]
 ROW3 = [(0, 0, k) for k in range(1, 4)]
 CHIPS3 = [(0, j, 0) for j in (2, 4, 6)]
@@ -79,7 +78,7 @@
            EU, MU, ZU, T16, T8, T4, X16, XB, GC, GS, S2, B2, A2, DG2, PD, RM, AP, XL,
            sem_in, s_e0, r_e0, s_c1z, r_c1z, s_c1, r_c1, s_e2, r_e2, s_uz, r_uz, s_u, r_u,
            s_ps, r_ps, s_gc1, r_gc1, s_gc2, r_gc2, s_gs1, r_gs1, s_gs2, r_gs2,
-           s_gc3, r_gc3, s_gc4, r_gc4, s_gs3, r_gs3, s_c1b, r_c1b,
+           s_gc3, r_gc3, s_gc4, r_gc4, s_gs3, r_gs3,
            s_z0, r_z0, s_mx, r_mx):
     gx, gy, gz = (lax.axis_index(a) for a in AXES)
     me = (gx, gy, gz)
@@ -149,7 +148,7 @@
         return pick(folded.reshape(64, 128), to_one).reshape(8, 8, 128)
 
     def restrict_two(sums):
-        T8[...] = sums
+        T8[0:4] = sums
         total = None
         for x in range(4):
             folded = T8[x, pl.ds(0, 4, stride=2), :] + T8[x, pl.ds(1, 4, stride=2), :]
@@ -299,11 +298,13 @@
     for n, (dx, dy, _) in enumerate(CORNERS):
         x, y = (2 if dx > 0 else 22), (4 if dy > 0 else 24)
         for a in range(4):
-            for k in range(4):
-                E0[a, x + k, pl.ds(y, 4), :] = CR[n, a, k // 2, pl.ds(4 * (k % 2), 4), :]
+            for k in range(2):
+                tile = CR[n, a, k]
+                E0[a, x + 2 * k, pl.ds(y, 4), :] = tile[0:4]
+                E0[a, x + 2 * k + 1, pl.ds(y, 4), :] = tile[4:8]
     wait(mx)
-    c1 = [send(C1.at[:, source_span(dx, 8, 8, 4), source_span(dy, 8, 8, 8)],
-               C1.at[:, target_span(dx, 8, 8, 4), target_span(dy, 8, 8, 8)],
+    c1 = [send(C1.at[:, source_span(dx, 8, 8, 8), source_span(dy, 8, 8, 8)],
+               C1.at[:, target_span(dx, 8, 8, 8), target_span(dy, 8, 8, 8)],
                s_c1.at[n], r_c1.at[n], (dx, dy, 0)) for n, (dx, dy, _) in enumerate(XY8)]
 
     lane32 = iota((32, 128), 1)
@@ -364,31 +365,7 @@
     for i in range(2, 10):
         red, black = residual_pair(V0, A0, FD0, DG0, 2, i, 4)
         sums.append((red + black)[4:20])
-    own = restrict_one(jnp.stack(sums))
-    wait(c1)
-
-    def pack1(p, carry):
-        xs = x1(p)
-        m = mask1[0][8:32] * xs
-        even, odd = C1[1, 2 * p - 2], C1[1, 2 * p - 1]
-        PB1[0, 0, p, pl.ds(8, 24), :] = jnp.where(q24, odd, even) * m
-        PB1[0, 1, p, pl.ds(8, 24), :] = jnp.where(q24, even, odd) * m
-        even, odd = C1[0, 2 * p - 2], C1[0, 2 * p - 1]
-        DG1[0, 0, p - 1] = jnp.where(q24, odd, even)
-        DG1[0, 1, p - 1] = jnp.where(q24, even, odd)
-        return carry
-
-    def coefficients1(lo, hi):
-        loop(lo + 1, hi + 1, pack1, 0, 4)
-        coefficients(PB1, A1, D1, DG1, 1, 8, 0.25, lambda t, c, i: DG1[t, c, i], mask1, x1, lo, hi)
-
-    coefficients1(2, 10)
-    q8 = (iota((8, 128), 0) + iota((8, 128), 1)) % 2 == 1
-    for i in range(4, 8):
-        even, odd = own[2 * i - 8], own[2 * i - 7]
-        red = jnp.where(q8, odd, even) * D1[0, 0, i, pl.ds(8, 8), :]
-        black = jnp.where(q8, even, odd) * D1[0, 1, i, pl.ds(8, 8), :]
-        S1[2 * i, pl.ds(8, 8)], S1[2 * i + 1, pl.ds(8, 8)] = unpack(red, black, q8)
+    S1[pl.ds(8, 8), pl.ds(8, 8)] = restrict_one(jnp.stack(sums))
     slot = iota((8, 128), 1) // 16
     for g in range(2):
         total = jnp.zeros((8, 128), F32)
@@ -421,9 +398,24 @@
     wait(gc2)
     row_of = GC.at[pl.ds(gy * 4, 4)]
     gc3 = [send(row_of, row_of, s_gc3.at[n], r_gc3.at[n], o) for n, o in enumerate(CHIPS3)]
-    c1b = [send(C1.at[:, source_span(-dx, 8, 8, 4), source_span(dy, 8, 8, 8)],
-                C1.at[:, pl.ds(0 if dx > 0 else 20, 4), target_span(dy, 8, 8, 8)],
-                s_c1b.at[n], r_c1b.at[n], (dx, dy, 0)) for n, (dx, dy, _) in enumerate(X6)]
+    wait(c1)
+
+    def pack1(p, carry):
+        xs = x1(p)
+        m = mask1[0][8:32] * xs
+        even, odd = C1[1, 2 * p - 2], C1[1, 2 * p - 1]
+        PB1[0, 0, p, pl.ds(8, 24), :] = jnp.where(q24, odd, even) * m
+        PB1[0, 1, p, pl.ds(8, 24), :] = jnp.where(q24, even, odd) * m
+        even, odd = C1[0, 2 * p - 2], C1[0, 2 * p - 1]
+        DG1[0, 0, p - 1] = jnp.where(q24, odd, even)
+        DG1[0, 1, p - 1] = jnp.where(q24, even, odd)
+        return carry
+
+    def coefficients1(lo, hi):
+        loop(lo + 1, hi + 1, pack1, 0, 4)
+        coefficients(PB1, A1, D1, DG1, 1, 8, 0.25, lambda t, c, i: DG1[t, c, i], mask1, x1, lo, hi)
+
+    coefficients1(0, 12)
     wait(e2)
     slot24 = lane24 // 16
     for x in range(4, 20):
@@ -436,9 +428,8 @@
     def rhs1(source, lo, hi):
         def body(i, carry):
             even, odd = source[2 * i], source[2 * i + 1]
-            m = mask1[0][8:32] * x1(i + 1)
-            FD1[0, 0, i] = jnp.where(q24, odd, even) * m
-            FD1[0, 1, i] = jnp.where(q24, even, odd) * m
+            FD1[0, 0, i] = jnp.where(q24, odd, even) * D1[0, 0, i]
+            FD1[0, 1, i] = jnp.where(q24, even, odd) * D1[0, 1, i]
             return carry
         loop(lo, hi, body, 0, 4)
 
@@ -458,6 +449,7 @@
     for n in range(4):
         rows = GC.at[pl.ds((core + 2 * n) * 4, 4)]
         gc4.append(send(rows, rows, s_gc4.at[n], r_gc4.at[n]))
+    q8 = (iota((8, 128), 0) + iota((8, 128), 1)) % 2 == 1
     for i in range(4, 8):
         red, black = V1[0, 0, i + 1, pl.ds(16, 8), :], V1[0, 1, i + 1, pl.ds(16, 8), :]
         PS[0, 2 * i, pl.ds(8, 8)], PS[0, 2 * i + 1, pl.ds(8, 8)] = unpack(red, black, q8)
@@ -526,8 +518,6 @@
 
     loop(0, 32, weights2, 0, 8)
 
-    wait(c1b)
-    coefficients1(0, 12)
 
     for n, (_, j, k) in enumerate(SAME15):
         gs2[n].wait()
@@ -684,13 +674,13 @@
     vmem(1, 2, 14, 40, 128), vmem(1, 2, 14, 40, 128), vmem(1, 2, 6, 12, 24, 128),
     vmem(1, 2, 12, 24, 128), vmem(1, 2, 12, 24, 128), vmem(1, 2, 12, 24, 128),
     vmem(2, 28, 32, 128), vmem(2, 16, 128), vmem(2, 2, 16, 128),
-    vmem(8, 16, 128), vmem(4, 8, 128), vmem(4, 8, 128), vmem(12, 32, 128), vmem(14, 32, 128),
-    vmem(32, 8, 2, 4, 128), vmem(32, 8, 4, 128),
+    vmem(8, 16, 128), vmem(6, 8, 128), vmem(4, 8, 128), vmem(12, 32, 128), vmem(14, 32, 128),
+    vmem(33, 8, 2, 4, 128), vmem(33, 8, 4, 128),
     vmem(32, 32, 128), vmem(40, 48, 128), vmem(6, 32, 32, 128), vmem(32, 32, 128),
     vmem(40, 48, 128), vmem(33, 32, 128), vmem(32, 32, 128), vmem(12, 16, 128),
     dma(4), dma(8), dma(8), dma(2), dma(2), dma(8), dma(8), dma(26), dma(26), dma(2), dma(2), dma(8), dma(8),
     dma(8), dma(8), dma(7), dma(7), dma(3), dma(3), dma(7), dma(7), dma(15), dma(15),
-    dma(3), dma(3), dma(4), dma(4), dma(16), dma(16), dma(6), dma(6),
+    dma(3), dma(3), dma(4), dma(4), dma(16), dma(16),
     dma(2), dma(2), dma(8), dma(8),
 ]
 

time: 59.4 us -> 57.3 us (0.965)
  Pallas kernels: 56.4 us -> 54.3 us
    pallas_call x1, Pallas kernels: 56.4 us -> 54.3 us  [local(): pl.pallas_call(kernel, out_shape=(shape, shape), in_specs=[pl.BlockSpec(m...]
where the time goes in v5:
time: 57.3 us; the launch traced here: 57.2 us
  Pallas kernels  54.3 us (95%)
  local copies, waits for them, and re-layouts  2.26 us (4%)
  between operations  0.65 us (1%)
    pallas_call x1, Pallas kernels, local(): pl.pallas_call(kernel, out_shape=(shape, shape), in_specs=[pl.BlockSpec(m...  54.3 us
    unnamed x4, local copies, waits for them, and re-layouts  2.26 us

profile of v5, /device:TPU:1, one launch (start us, length us, event | category | flops | bytes accessed | tf_op | source)
XLA Modules:
  0.0 57.2 jit_solution(8188142972814369777)
XLA Ops:
  0.6 54.3 %shard_map.59 = (f32[16,16,128]{2,1,0:T(8,128)}, f32[16,16,128]{2,1,0:T(8,128)}) custom-call(f32[16,16,128]{2,1,0:T(8,128)} %f_in.1, f32[16,16,128]{2,1,0:T(8,128)} %u_in.1, f32[16,16,128]{2,1,0:T(8,128)} %s_in.1, f32[16,16,128]{2,1,0:T(8,128)} %b_in.1), custom_call_target="tpu_custom_call" | custom-call | tf_op jit(solution)/shard_map/pallas_call | solution.py:691
  55.0 0.0 copy-start
  55.0 1.6 %copy.8 = f32[16,16,128]{2,1,0:T(8,128)} copy(f32[16,16,128]{2,1,0:T(8,128)} %get-tuple-element.4) | data formatting | bytes 262144
  56.6 0.0 copy-done
  56.6 0.7 %copy.9 = f32[16,16,128]{2,1,0:T(8,128)} copy(f32[16,16,128]{2,1,0:T(8,128)S(1)} %copy-done) | data formatting | bytes 262144
Async XLA Ops:
  55.0 1.6 %copy-start = (f32[16,16,128]{2,1,0:T(8,128)S(1)}, f32[16,16,128]{2,1,0:T(8,128)}, u32[]{:S(2)}) copy-start(f32[16,16,128]{2,1,0:T(8,128)} %get-tuple-element.5) | copy-start | bytes 393220

commit v6 on v5

--- a/solution.py
+++ b/solution.py
@@ -523,10 +523,10 @@
         gs2[n].wait()
         came = GS.at[lax.rem(gy + 8 - j, 8) * 4 + lax.rem(gz + 4 - k, 4)]
         gs3.append(send(came, came, s_gs3.at[n], r_gs3.at[n]))
-    wait(gs3)
     eu = [send(EU.at[:, source_span(dx, 6, 16, 5), source_span(dy, 8, 16, 8)],
                EU.at[:, target_span(dx, 6, 16, 5), target_span(dy, 8, 16, 8)],
                s_u.at[n], r_u.at[n], (dx, dy, 0)) for n, (dx, dy, _) in enumerate(XY8)]
+    wait(gs3)
     spread(lambda j, g: GS[j, g], store_source)
     XL[...] = jnp.zeros_like(XL)
 

time: 57.3 us -> 57.1 us (level)
  no operation moved by 1% of the time
where the time goes in v6:
time: 57.1 us; the launch traced here: 57 us
  Pallas kernels  54.1 us (95%)
  local copies, waits for them, and re-layouts  2.26 us (4%)
  between operations  0.65 us (1%)
    pallas_call x1, Pallas kernels, local(): pl.pallas_call(kernel, out_shape=(shape, shape), in_specs=[pl.BlockSpec(m...  54.1 us
    unnamed x4, local copies, waits for them, and re-layouts  2.26 us

profile of v6, /device:TPU:1, one launch (start us, length us, event | category | flops | bytes accessed | tf_op | source)
XLA Modules:
  0.0 57.0 jit_solution(3666600230510907636)
XLA Ops:
  0.6 54.1 %shard_map.59 = (f32[16,16,128]{2,1,0:T(8,128)}, f32[16,16,128]{2,1,0:T(8,128)}) custom-call(f32[16,16,128]{2,1,0:T(8,128)} %f_in.1, f32[16,16,128]{2,1,0:T(8,128)} %u_in.1, f32[16,16,128]{2,1,0:T(8,128)} %s_in.1, f32[16,16,128]{2,1,0:T(8,128)} %b_in.1), custom_call_target="tpu_custom_call" | custom-call | tf_op jit(solution)/shard_map/pallas_call | solution.py:691
  54.7 0.0 copy-start
  54.7 1.6 %copy.8 = f32[16,16,128]{2,1,0:T(8,128)} copy(f32[16,16,128]{2,1,0:T(8,128)} %get-tuple-element.4) | data formatting | bytes 262144
  56.3 0.0 copy-done
  56.3 0.7 %copy.9 = f32[16,16,128]{2,1,0:T(8,128)} copy(f32[16,16,128]{2,1,0:T(8,128)S(1)} %copy-done) | data formatting | bytes 262144
Async XLA Ops:
  54.7 1.6 %copy-start = (f32[16,16,128]{2,1,0:T(8,128)S(1)}, f32[16,16,128]{2,1,0:T(8,128)}, u32[]{:S(2)}) copy-start(f32[16,16,128]{2,1,0:T(8,128)} %get-tuple-element.5) | copy-start | bytes 393220
